TPU v7x, 32 devices: a whole 2x2x4 slice. The times are simulated.
32 devices in a mesh: search: 16 (over z, y, x), mp: 2 (over core).
Axes of the slice: x: 2, y: 2, z: 4, core: 2. Of those that a mesh axis runs over, the one named last changes fastest.
Arguments:
- queries: bfloat16 [256, 2, 128, 192], P('search', None, 'mp'), may hold values from -240 to 240
- new_latents: bfloat16 [256, 2, 576], P('search'), may hold values from -6 to 6
- parent_cache: bfloat16 [16, 4096, 576], P('search'), may hold values from -4 to 4
- parent_of: int32 [256], P('search'), may hold values from 0 to 15, as said below
- up_keys: bfloat16 [128, 128, 512], P('mp'), may hold values from -0.5 to 0.5
- up_values: bfloat16 [128, 512, 128], P('mp'), may hold values from -0.25 to 0.25
- out_proj: bfloat16 [16384, 7168], P('mp', 'search'), may hold values from -0.0625 to 0.0625
- hidden_in: bfloat16 [256, 2, 7168], P('search', None, 'mp'), may hold values from -22 to 22
- router: bfloat16 [7168, 16], P('mp'), may hold values from -0.0625 to 0.0625
- routes: int32 [256, 2, 8], P('search'), may hold values from 0 to 15, all different within a row; in each aligned block of 32 rows (0 to 31, 32 to 63, ..., all dimensions but the last counted through in order) at most 24 rows name the same one
- w_gate: bfloat16 [16, 7168, 1024], P('search', None, 'mp'), may hold values from -0.0625 to 0.0625
- w_up: bfloat16 [16, 7168, 1024], P('search', None, 'mp'), may hold values from -0.0625 to 0.0625
- w_down: bfloat16 [16, 1024, 7168], P('search', 'mp'), may hold values from -0.25 to 0.25
Outputs:
- mixed: bfloat16 [256, 2, 7168], P('search', None, 'mp')
Inputs may be any that keep to these rules, and one draw needn't show every extreme that they name: `parent_of`: the children of one device fall into 8 groups of 2 children with a common parent, the groups' parents all different; every parent has 16 children. `routes`: each row names 8 different experts; in the rows of one device no expert is named more than 24 times, and that most is reached.
All inputs are finite; a program needn't handle non-finite values.
Results may differ from a plain program's by a relative error of at most 0.017.
Values may be sent and summed in bfloat16 or wider, within the bound.
A program may use at most 192 MiB of HBM per device.

v0:
```python
import jax
import jax.numpy as jnp
from jax import lax
from jax.sharding import PartitionSpec as P

D = 7168


def slot_table(targets, buckets, per_bucket):
    onehot = (targets[:, None] == jnp.arange(buckets, dtype=jnp.int32)[None, :]).astype(jnp.int32)
    earlier = jnp.cumsum(onehot, axis=0) - onehot
    ranking = jnp.sum(earlier * onehot, axis=1)
    return targets * per_bucket + ranking


def relocate(placer, values, lead_shape):
    flat = values.reshape(values.shape[0], -1)
    moved = jnp.dot(placer, flat, preferred_element_type=jnp.float32).astype(values.dtype)
    return moved.reshape(lead_shape + values.shape[1:])


def absorb(query_block, up_keys, nope_width):
    latent_query = jnp.einsum(
        "...hn,hnl->...hl",
        query_block[..., :nope_width],
        up_keys,
        preferred_element_type=jnp.float32,
    ).astype(jnp.bfloat16)
    return jnp.concatenate([latent_query, query_block[..., nope_width:]], axis=-1)


def prefix_scores(query_rows, prefix_cache, softmax_scale):
    return (
        lax.dot_general(
            query_rows, prefix_cache, (((1,), (1,)), ((), ())), preferred_element_type=jnp.float32
        )
        * softmax_scale
    )


def own_scores_of(full_query, own_keys, softmax_scale, causal):
    raw_scores = (
        jnp.einsum("cthk,cuk->cthu", full_query, own_keys, preferred_element_type=jnp.float32)
        * softmax_scale
    )
    return jnp.where(causal[:, None, :], raw_scores, -jnp.inf)


def local(
    queries,
    new_latents,
    parent_cache,
    parent_of,
    up_keys,
    up_values,
    out_proj,
    hidden_in,
    router,
    routes,
    w_gate,
    w_up,
    w_down,
):
    searchers = lax.axis_size("search")
    children_here, new_tokens, heads_here, query_width = queries.shape
    nope_width = up_keys.shape[1]
    latent_width = up_keys.shape[2]
    kv_width = parent_cache.shape[2]
    value_width = up_values.shape[2]
    softmax_scale = float(query_width) ** (-0.5)
    pair_slots = children_here // (searchers // 2)
    slots_total = searchers * pair_slots
    slot_ids = slot_table(parent_of, searchers, pair_slots)
    placer = (jnp.arange(slots_total, dtype=jnp.int32)[:, None] == slot_ids[None, :]).astype(
        jnp.bfloat16
    )
    prefix_cache = parent_cache[0]
    causal = jnp.arange(new_tokens)[None, :] <= jnp.arange(new_tokens)[:, None]
    lead_shape = (searchers, pair_slots)
    full_query = absorb(queries, up_keys, nope_width)
    outgoing = relocate(placer, full_query, lead_shape)
    arrived = lax.all_to_all(outgoing, "search", split_axis=0, concat_axis=0, tiled=True)
    scores = prefix_scores(arrived.reshape(-1, kv_width), prefix_cache, softmax_scale)
    row_peak = jnp.max(scores, axis=1)
    weights = jnp.exp(scores - row_peak[:, None])
    row_mass = jnp.sum(weights, axis=1)
    summed = jnp.dot(
        weights.astype(jnp.bfloat16),
        prefix_cache[:, :latent_width],
        preferred_element_type=jnp.float32,
    )
    back_shape = lead_shape + (new_tokens, heads_here)
    back_peak, back_mass, back_sum = (
        lax.all_to_all(
            row_peak.reshape(back_shape).astype(jnp.bfloat16),
            "search",
            split_axis=0,
            concat_axis=0,
            tiled=True,
        ).astype(jnp.float32),
        lax.all_to_all(
            row_mass.reshape(back_shape).astype(jnp.bfloat16),
            "search",
            split_axis=0,
            concat_axis=0,
            tiled=True,
        ).astype(jnp.float32),
        lax.all_to_all(
            summed.reshape(back_shape + (latent_width,)).astype(jnp.bfloat16),
            "search",
            split_axis=0,
            concat_axis=0,
            tiled=True,
        ).astype(jnp.float32),
    )
    far_peak = jnp.take(back_peak.reshape(slots_total, new_tokens, heads_here), slot_ids, axis=0)
    far_mass = jnp.take(back_mass.reshape(slots_total, new_tokens, heads_here), slot_ids, axis=0)
    far_sum = jnp.take(
        back_sum.reshape(slots_total, new_tokens, heads_here, latent_width), slot_ids, axis=0
    )
    own_scores = own_scores_of(full_query, new_latents, softmax_scale, causal)
    top_score = jnp.maximum(far_peak, jnp.max(own_scores, axis=-1))
    own_weights = jnp.exp(own_scores - top_score[..., None])
    factor = jnp.exp(far_peak - top_score)
    denominator = far_mass * factor + jnp.sum(own_weights, axis=-1)
    numerator = far_sum * factor[..., None] + jnp.einsum(
        "cthu,cul->cthl",
        own_weights.astype(jnp.bfloat16),
        new_latents[..., :latent_width],
        preferred_element_type=jnp.float32,
    )
    latent_out = (numerator / denominator[..., None]).astype(jnp.bfloat16)
    head_out = jnp.einsum(
        "cthl,hlv->cthv", latent_out, up_values, preferred_element_type=jnp.float32
    ).astype(jnp.bfloat16)
    token_rows = children_here * new_tokens
    attention = head_out.reshape(token_rows, heads_here * value_width)
    every_row = jnp.dot(
        lax.all_gather(attention, "search", axis=0, tiled=True),
        out_proj,
        preferred_element_type=jnp.float32,
    )
    owned = lax.all_to_all(
        every_row.astype(jnp.bfloat16), "search", split_axis=0, concat_axis=1, tiled=True
    ).astype(every_row.dtype)
    projected = lax.psum_scatter(
        owned.astype(jnp.bfloat16), "mp", scatter_dimension=1, tiled=True
    ).astype(jnp.float32)
    width_here = hidden_in.shape[2]
    residual = (hidden_in.reshape(token_rows, width_here).astype(jnp.float32) + projected).astype(
        jnp.bfloat16
    )
    residual_wide = residual.astype(jnp.float32)
    squares = jnp.sum(residual_wide * residual_wide, axis=1)
    router_part = jnp.dot(residual, router, preferred_element_type=jnp.float32)
    squares, router_part = lax.psum((squares, router_part), "mp")
    inv_rms = lax.rsqrt(squares / D + 1e-06)
    logits = router_part * inv_rms[:, None]
    normed = (residual_wide * inv_rms[:, None]).astype(jnp.bfloat16)
    picked = routes.reshape(token_rows, -1)
    topk_here = picked.shape[1]
    experts_total = router.shape[1]
    affinity = jax.nn.sigmoid(logits)
    expert_range = jnp.arange(experts_total, dtype=jnp.int32)
    chosen = jnp.sum(
        jnp.where(picked[:, :, None] == expert_range[None, None, :], affinity[:, None, :], 0.0),
        axis=2,
    )
    gate_weights = 2.5 * chosen / jnp.sum(chosen, axis=1, keepdims=True)
    capacity = min(token_rows, 3 * token_rows * topk_here // (2 * experts_total))
    expert_slots = slot_table(picked.reshape(-1), experts_total, capacity).reshape(
        token_rows, topk_here
    )
    slot_range = jnp.arange(experts_total * capacity, dtype=jnp.int32)
    dispatch_matrix = jnp.any(slot_range[:, None, None] == expert_slots[None, :, :], axis=2).astype(
        jnp.bfloat16
    )
    outgoing = jnp.dot(dispatch_matrix, normed, preferred_element_type=jnp.float32).astype(
        jnp.bfloat16
    )
    arrived = lax.all_to_all(
        outgoing.reshape(experts_total, capacity, width_here),
        "search",
        split_axis=0,
        concat_axis=0,
        tiled=True,
    )
    arrived = arrived.reshape(searchers * capacity, width_here)
    gate_weight = w_gate[0]
    up_weight = w_up[0]
    shard_piece = lax.all_gather(arrived, "mp", axis=1, tiled=True)
    gate_act = jnp.dot(shard_piece, gate_weight, preferred_element_type=jnp.float32)
    up_act = jnp.dot(shard_piece, up_weight, preferred_element_type=jnp.float32)
    expert_hidden = (jax.nn.silu(gate_act) * up_act).astype(jnp.bfloat16)
    expert_out = lax.psum_scatter(
        jnp.dot(expert_hidden, w_down[0], preferred_element_type=jnp.float32).astype(jnp.bfloat16),
        "mp",
        scatter_dimension=1,
        tiled=True,
    ).astype(jnp.float32)
    returned = lax.all_to_all(
        expert_out.reshape(searchers, capacity, width_here).astype(jnp.bfloat16),
        "search",
        split_axis=0,
        concat_axis=0,
        tiled=True,
    ).astype(jnp.float32)
    gathered = jnp.take(
        returned.reshape(experts_total * capacity, width_here), expert_slots, axis=0
    )
    expert_mix = jnp.sum(gathered * gate_weights[:, :, None], axis=1)
    mixed = (residual_wide + expert_mix).astype(jnp.bfloat16)
    return mixed.reshape(children_here, new_tokens, width_here)


def solution(mesh):
    in_specs = (
        P("search", None, "mp", None),
        P("search", None, None),
        P("search", None, None),
        P("search"),
        P("mp", None, None),
        P("mp", None, None),
        P("mp", "search"),
        P("search", None, "mp"),
        P("mp", None),
        P("search", None, None),
        P("search", None, "mp"),
        P("search", None, "mp"),
        P("search", "mp", None),
    )
    out_specs = P("search", None, "mp")
    return jax.shard_map(local, mesh=mesh, in_specs=in_specs, out_specs=out_specs, check_vma=False)
```

profile of v0, /device:TPU:0, one launch (start us, length us, event | category | flops | bytes accessed | tf_op | source)
XLA Modules:
  0.0 742.4 jit_solution(1382252323568795714)
XLA Ops:
  11.4 4.8 convert_bitcast_fusion
  18.8 5.4 reshape.166
  24.2 5.2 convolution_convert_fusion
  29.4 8.8 %reshape.167 = bf16[16,2,2,64,576]{4,3,2,1,0:T(8,128)(2,1)} reshape(bf16[32,73728]{1,0:T(8,128)(2,1)} %convolution_convert_fusion) | data formatting | bytes 9437184 | tf_op jit(solution)/shard_map/reshape | solution.py:19
  38.2 124.8 %all_to_all.49 = bf16[16,2,2,64,576]{4,3,2,1,0:T(8,128)(2,1)} all-to-all(bf16[16,2,2,64,576]{4,3,2,1,0:T(8,128)(2,1)} %reshape.167), channel_id=1, replica_groups=mesh['search'=16,'mp'=2] {'search'}, dimensions={0} | all-to-all | bytes 9437184 | tf_op jit(solution)/shard_map/all_to_all | solution.py:82
  163.0 35.4 %multiply_reduce_fusion = (f32[4096]{0:T(1024)S(1)}, f32[4096,4096]{0,1:T(8,128)}) fusion(bf16[4096,576]{1,0:T(8,128)(2,1)} %bitcast.118, bf16[1,4096,576]{1,2,0:T(8,128)(2,1)} %param.17), kind=kOutput, calls=%fused_computation.6 | convolution fusion | flops 19360903168 | bytes 76562432 | tf_op jit(solution)/shard_map/dot_general | solution.py:34
  198.5 21.4 %fusion = bf16[4096]{0:T(1024)(128)(2,1)S(1)} fusion(f32[4096,4096]{0,1:T(8,128)} %get-tuple-element.19, f32[4096]{0:T(1024)S(1)} %get-tuple-element.18), kind=kLoop, calls=%fused_computation.7 | loop fusion | flops 50327552 | bytes 67133440 | tf_op jit(solution)/shard_map/reduce_sum | solution.py:86
  220.6 3.9 all-to-all-start.3
  225.3 6.5 all-to-all-done.3
  231.8 3.7 all-to-all-start.2
  235.5 28.7 %fusion.15 = bf16[4096,512]{1,0:T(8,128)(2,1)} fusion(f32[4096,4096]{0,1:T(8,128)} %get-tuple-element.19, f32[4096]{0:T(1024)S(1)} %get-tuple-element.18, bf16[4096,576]{0,1:T(8,128)(2,1)} %bitcast.128), kind=kOutput, calls=%fused_computation.22 | convolution fusion | flops 17232297984 | bytes 75513856 | tf_op jit(solution)/shard_map/dot_general | solution.py:87
  264.2 7.2 all-to-all-start.1
  274.5 74.2 %all-to-all-done.1 = bf16[16,2,2,64,512]{4,3,2,1,0:T(8,128)(2,1)} async-done(((bf16[16,2,2,64,512]{4,3,2,1,0:T(8,128)(2,1)}), bf16[16,2,2,64,512]{4,3,2,1,0:T(8,128)(2,1)}, u32[]{:S(2)}, u32[]{:S(2)}) %all-to-all-start.1) | async-done | bytes 4194336 | tf_op jit(solution)/shard_map/all_to_all | solution.py:108
  348.7 6.6 bitcast_convert_fusion
  355.3 6.2 gather_fusion
  361.5 2.9 divide_convert_fusion
  364.4 5.4 fusion.35
  371.7 125.0 %all-gather.3.cloned.1.call-done = bf16[512,8192]{1,0:T(8,128)(2,1)} async-done(((bf16[32,8192]{1,0:T(8,128)(2,1)}), bf16[512,8192]{1,0:T(8,128)(2,1)}) %all-gather.3.cloned.1.call-update) | async-done | bytes 8388624 | tf_op jit(solution)/shard_map/all_gather | solution.py:139
  496.7 9.4 %convolution_convert_fusion.3 = bf16[512,448]{0,1:T(8,128)(2,1)S(1)} fusion(bf16[512,8192]{1,0:T(8,128)(2,1)} %all-gather.3.cloned.1.call-done, bf16[8192,448]{0,1:T(8,128)(2,1)} %param.21), kind=kOutput, calls=%fused_computation.36 | convolution fusion | flops 3758325760 | bytes 16187392 | tf_op jit(solution)/shard_map/dot_general | solution.py:138
  506.4 18.8 %all_to_all.50 = bf16[16,32,448]{2,1,0:T(8,128)(2,1)S(1)} all-to-all(bf16[16,32,448]{2,1,0:T(8,128)(2,1)S(1)} %bitcast.123), channel_id=1, replica_groups=mesh['search'=16,'mp'=2] {'search'}, dimensions={0} | all-to-all | bytes 917504 | tf_op jit(solution)/shard_map/all_to_all | solution.py:143
  528.5 4.7 reduce-scatter.3.cloned.1.call-done
  534.5 2.5 all-reduce
  537.9 70.8 %all_to_all.51 = bf16[16,24,3584]{2,1,0:T(8,128)(2,1)} all-to-all(bf16[16,24,3584]{2,1,0:T(8,128)(2,1)S(1)} %bitcast.117), channel_id=1, replica_groups=mesh['search'=16,'mp'=2] {'search'}, dimensions={0} | all-to-all | bytes 5505024 | tf_op jit(solution)/shard_map/all_to_all | solution.py:181
  609.0 13.0 %all-gather.5.cloned.1.call-done = bf16[384,7168]{1,0:T(8,128)(2,1)} async-done(((bf16[384,3584]{1,0:T(8,128)(2,1)}), bf16[384,7168]{1,0:T(8,128)(2,1)}) %all-gather.5.cloned.1.call-update) | async-done | bytes 5505040 | tf_op jit(solution)/shard_map/all_gather | solution.py:191
  622.0 6.9 fusion.13
  629.0 15.2 %convolution_convert_fusion.1 = bf16[384,7168]{1,0:T(8,128)(2,1)} fusion(bf16[1,512,7168]{2,1,0:T(8,128)(2,1)} %param.27, bf16[384,7168]{1,0:T(8,128)(2,1)} %all-gather.5.cloned.1.call-done, bf16[1,7168,512]{2,1,0:T(8,128)(2,1)} %param.26, f32[384,512]{1,0:T(8,128)S(1)} %fusion.13), kind=kOutput, calls=%fused_computation.12 | convolution fusion | flops 5641076736 | bytes 26476544 | tf_op jit(solution)/shard_map/dot_general | solution.py:196
  644.2 14.8 %reduce-scatter.5.cloned.1.call-done = bf16[384,3584]{1,0:T(8,128)(2,1)} async-done(((bf16[384,7168]{1,0:T(8,128)(2,1)}), bf16[384,3584]{1,0:T(8,128)(2,1)}) %reduce-scatter.5.cloned.1.call-update) | async-done | bytes 2752528 | tf_op jit(solution)/shard_map/reduce_scatter | solution.py:195
  659.0 6.8 all-to-all-start.6
  666.4 53.9 %all-to-all-done.6 = bf16[16,24,3584]{2,1,0:T(8,128)(2,1)S(1)} async-done(((bf16[16,24,3584]{2,1,0:T(8,128)(2,1)}), bf16[16,24,3584]{2,1,0:T(8,128)(2,1)S(1)}, u32[]{:S(2)}, u32[]{:S(2)}) %all-to-all-start.6) | async-done | bytes 2752544 | tf_op jit(solution)/shard_map/all_to_all | solution.py:201
  720.2 3.2 bitcast_convert_fusion.1
  723.5 7.8 %gather_fusion.1 = f32[256,3584]{1,0:T(8,128)} fusion(f32[384,3584]{1,0:T(8,128)} %bitcast_convert_fusion.1, s32[1024]{0:T(1024)S(1)} %pad_clamp_fusion), kind=kCustom, calls=%fused_computation.3 | custom fusion | bytes 7341056 | tf_op jit(solution)/shard_map/jit(_take)/gather | solution.py:208
  731.3 3.5 fusion.20
  (79 shorter events, 21.2 us)
Async XLA Ops:
  6.5 527.8 %copy-start = (bf16[3584,16]{0,1:T(8,128)(2,1)S(1)}, bf16[3584,16]{0,1:T(8,128)(2,1)}, u32[]{:S(2)}) copy-start(bf16[3584,16]{0,1:T(8,128)(2,1)} %param.23) | copy-start | bytes 344068
  220.6 11.2 %all-to-all-start.3 = ((bf16[16,2,128]{2,1,0:T(2,128)(2,1)}), bf16[16,2,128]{2,1,0:T(2,128)(2,1)S(1)}, u32[]{:S(2)}, u32[]{:S(2)}) async-start(bf16[16,2,128]{2,1,0:T(2,128)(2,1)} %reshape.238), calls=%async_computation.3 | async-start | bytes 16384 | tf_op jit(solution)/shard_map/all_to_all | solution.py:101
  231.8 32.4 %all-to-all-start.2 = ((bf16[16,2,128]{2,1,0:T(2,128)(2,1)}), bf16[16,2,128]{2,1,0:T(2,128)(2,1)S(1)}, u32[]{:S(2)}, u32[]{:S(2)}) async-start(bf16[16,2,128]{2,1,0:T(2,128)(2,1)} %reshape.236), calls=%async_computation.2 | async-start | bytes 16384 | tf_op jit(solution)/shard_map/all_to_all | solution.py:94
  264.2 7.3 copy-start.3
  264.2 84.5 %all-to-all-start.1 = ((bf16[16,2,2,64,512]{4,3,2,1,0:T(8,128)(2,1)}), bf16[16,2,2,64,512]{4,3,2,1,0:T(8,128)(2,1)}, u32[]{:S(2)}, u32[]{:S(2)}) async-start(bf16[16,2,2,64,512]{4,3,2,1,0:T(8,128)(2,1)} %bitcast.119), calls=%async_computation.1 | async-start | bytes 8388608 | tf_op jit(solution)/shard_map/all_to_all | solution.py:108
  271.3 225.4 %all-gather.3.cloned.1.call-start = ((), (), s32[]{:S(2)}) async-start(), calls=%async_computation.9 | async-start | bytes 8912896 | tf_op jit(solution)/shard_map/all_gather | solution.py:139
  371.2 155.7 %copy-start.2 = (s32[16,2,8]{0,2,1:T(8,128)S(1)}, s32[16,2,8]{0,2,1:T(8,128)}, u32[]{:S(2)}) copy-start(s32[16,2,8]{0,2,1:T(8,128)} %param.24) | copy-start | bytes 3076
  371.2 157.0 %copy-start.1 = (bf16[16,2,3584]{2,1,0:T(2,128)(2,1)S(1)}, bf16[16,2,3584]{2,1,0:T(2,128)(2,1)}, u32[]{:S(2)}) copy-start(bf16[16,2,3584]{2,1,0:T(2,128)(2,1)} %param.22) | copy-start | bytes 688132
  371.2 162.0 %reduce-scatter.3.cloned.1.call-start = ((), (), s32[]{:S(2)}) async-start(), calls=%async_computation.10 | async-start | bytes 688128 | tf_op jit(solution)/shard_map/reduce_scatter | solution.py:146
  526.9 95.2 %all-gather.5.cloned.1.call-start = ((), (), s32[]{:S(2)}) async-start(), calls=%async_computation.11 | async-start | bytes 8257536 | tf_op jit(solution)/shard_map/all_gather | solution.py:191
  608.8 50.2 %reduce-scatter.5.cloned.1.call-start = ((), (), s32[]{:S(2)}) async-start(), calls=%async_computation.12 | async-start | bytes 8257536 | tf_op jit(solution)/shard_map/reduce_scatter | solution.py:195
  659.0 61.2 %all-to-all-start.6 = ((bf16[16,24,3584]{2,1,0:T(8,128)(2,1)}), bf16[16,24,3584]{2,1,0:T(8,128)(2,1)S(1)}, u32[]{:S(2)}, u32[]{:S(2)}) async-start(bf16[16,24,3584]{2,1,0:T(8,128)(2,1)} %bitcast.120), calls=%async_computation.8 | async-start | bytes 5505024 | tf_op jit(solution)/shard_map/all_to_all | solution.py:201
Sparse Core Ops, SparseCore 0:
  371.3 125.3 all-gather.2
  527.0 6.1 reduce-scatter.2
  608.9 13.0 all-gather.4
  644.3 14.6 reduce-scatter.4
where the time goes:
time: 757 us; the launch traced here: 742 us
  waiting for transfers between devices  292 us (39%)
  blocking collectives  217 us (29%)
  matrix products  116 us (15%)
  local copies, waits for them, and re-layouts  41 us (5%)
  other arithmetic  39.9 us (5%)
  starting transfers between devices  22.3 us (3%)
  between operations  13.7 us (2%)
    all_gather x1, waiting for transfers between devices, local(): lax.all_gather(attention, 'search', axis=0, tiled=True)  125 us
    all_to_all x1, blocking collectives, local(): lax.all_to_all(outgoing, 'search', split_axis=0, concat_axis=0, tiled=True)  125 us
    all_to_all x1, waiting for transfers between devices, local(): lax.all_to_all(summed.reshape(back_shape + (latent_width,)).astype(jnp.bf...  74.2 us
    all_to_all x1, blocking collectives, local(): lax.all_to_all(outgoing.reshape(experts_total, capacity, width_here), 'se...  70.8 us
    all_to_all x1, waiting for transfers between devices, local(): lax.all_to_all(expert_out.reshape(searchers, capacity, width_here).astype...  53.9 us
    dot_general x1, matrix products, prefix_scores(): lax.dot_general(query_rows, prefix_cache, (((1,), (1,)), ((), ())), prefe...  35.4 us
    dot_general x1, matrix products, local(): jnp.dot(weights.astype(jnp.bfloat16), prefix_cache[:, :latent_width], pre...  28.7 us
    reduce_sum x1, other arithmetic, local(): row_mass = jnp.sum(weights, axis=1)  21.4 us
  transfers between devices with their start and end apart: 8, of which 7 were waited for; matrix products, arithmetic and copies ran while one was open for 5% of the time, Pallas kernels for 0%

commit v1 on v0

v1 whole, which is shorter than its diff:
```python
import functools

import jax
import jax.numpy as jnp
from jax import lax
from jax.experimental import pallas as pl
from jax.experimental.pallas import tpu as pltpu
from jax.sharding import PartitionSpec as P

D = 7168
BF16, F32, I32 = jnp.bfloat16, jnp.float32, jnp.int32


def attend_kernel(tile_children, heads, softmax_scale, latent_width, key_chunk,
                  query_ref, own_ref, cache_ref, out_ref, scores_ref):
    rows = query_ref.shape[0]
    prefix = cache_ref.shape[0]
    query = query_ref[...]
    nt = (((1,), (1,)), ((), ()))
    own = own_ref[...]
    own_count = own.shape[0]
    own_scores = lax.dot_general(query, own, nt, preferred_element_type=F32) * softmax_scale
    row_id = lax.broadcasted_iota(I32, (rows, own_count), 0) // heads
    key_id = lax.broadcasted_iota(I32, (rows, own_count), 1)
    steps = own_count // tile_children
    visible = (row_id // steps == key_id // steps) & (key_id % steps <= row_id % steps)
    own_scores = jnp.where(visible, own_scores, -jnp.inf)
    peak = jnp.max(own_scores, axis=1, keepdims=True)
    for start in range(0, prefix, key_chunk):
        chunk = lax.dot_general(
            query, cache_ref[pl.ds(start, key_chunk), :], nt, preferred_element_type=F32
        ) * softmax_scale
        scores_ref[:, pl.ds(start, key_chunk)] = chunk
        peak = jnp.maximum(peak, jnp.max(chunk, axis=1, keepdims=True))
    own_weights = jnp.exp(own_scores - peak)
    mass = jnp.sum(own_weights, axis=1, keepdims=True)
    total = jnp.dot(own_weights.astype(BF16), own[:, :latent_width], preferred_element_type=F32)
    for start in range(0, prefix, key_chunk):
        weights = jnp.exp(scores_ref[:, pl.ds(start, key_chunk)] - peak)
        mass = mass + jnp.sum(weights, axis=1, keepdims=True)
        total = total + jnp.dot(
            weights.astype(BF16),
            cache_ref[pl.ds(start, key_chunk), :latent_width],
            preferred_element_type=F32,
        )
    out_ref[...] = (total / mass).astype(BF16)


def attend(full_query, own_latents, prefix_cache, latent_width, softmax_scale):
    children, steps, heads, kv_width = full_query.shape
    tile_children = max(1, min(children, 512 // (steps * heads)))
    rows = tile_children * steps * heads
    prefix = prefix_cache.shape[0]
    tiles = children // tile_children
    body = functools.partial(attend_kernel, tile_children, heads, softmax_scale, latent_width, min(1024, prefix))
    own_rows = tile_children * steps
    own_tiles = own_latents.reshape(tiles, own_rows, kv_width)
    out = pl.pallas_call(
        body,
        grid=(tiles,),
        in_specs=[
            pl.BlockSpec((rows, kv_width), lambda i: (i, 0)),
            pl.BlockSpec((pl.squeezed, own_rows, kv_width), lambda i: (i, 0, 0)),
            pl.BlockSpec((prefix, kv_width), lambda i: (0, 0)),
        ],
        out_specs=pl.BlockSpec((rows, latent_width), lambda i: (i, 0)),
        out_shape=jax.ShapeDtypeStruct((tiles * rows, latent_width), BF16),
        scratch_shapes=[pltpu.VMEM((rows, prefix), F32)],
        compiler_params=pltpu.CompilerParams(vmem_limit_bytes=52 * 1024 * 1024),
        cost_estimate=pl.CostEstimate(
            flops=2 * tiles * rows * prefix * (kv_width + latent_width),
            bytes_accessed=2 * (tiles * rows * (kv_width + latent_width) + prefix * kv_width),
            transcendentals=tiles * rows * prefix,
        ),
        name="attend",
    )(full_query.reshape(tiles * rows, kv_width), own_tiles, prefix_cache)
    return out.reshape(children, steps, heads, latent_width)


def local(
    queries,
    new_latents,
    parent_cache,
    parent_of,
    up_keys,
    up_values,
    out_proj,
    hidden_in,
    router,
    routes,
    w_gate,
    w_up,
    w_down,
):
    searchers = lax.axis_size("search")
    me = lax.axis_index("search")
    children_here, new_tokens, heads_here, query_width = queries.shape
    nope_width = up_keys.shape[1]
    latent_width = up_keys.shape[2]
    kv_width = parent_cache.shape[2]
    value_width = up_values.shape[2]
    softmax_scale = float(query_width) ** (-0.5)
    pair_slots = children_here // (searchers // 2)
    children_all = searchers * children_here
    token_rows = children_here * new_tokens
    width_here = hidden_in.shape[2]

    parents = lax.all_gather(parent_of, "search", axis=0, tiled=True)
    ids = jnp.arange(children_all, dtype=I32)
    earlier_same = (parents[:, None] == parents[None, :]) & (ids[None, :] < ids[:, None])
    ranking = jnp.sum(earlier_same.astype(I32), axis=1)
    same_device = (ids[:, None] // children_here) == (ids[None, :] // children_here)
    pair_rank = jnp.sum((earlier_same & same_device).astype(I32), axis=1)
    position = parents * children_here + ranking
    arrival_slot = (ids // children_here) * pair_slots + pair_rank
    slots_total = searchers * pair_slots
    mine = me * children_here + jnp.arange(children_here, dtype=I32)
    taken = mine[:, None] == position[None, :]
    slot_of_mine = jnp.sum(jnp.where(taken, arrival_slot[None, :], 0), axis=1)
    picker = (slot_of_mine[:, None] == jnp.arange(slots_total, dtype=I32)[None, :]).astype(BF16)

    own_ids = jnp.arange(children_here, dtype=I32)
    own_rank = jnp.sum(
        ((parent_of[:, None] == parent_of[None, :]) & (own_ids[None, :] < own_ids[:, None])).astype(I32), axis=1
    )
    own_slot = parent_of * pair_slots + own_rank
    placer = (jnp.arange(slots_total, dtype=I32)[:, None] == own_slot[None, :]).astype(BF16)

    query_cols = new_tokens * heads_here * query_width
    payload = jnp.concatenate(
        [queries.reshape(children_here, -1), new_latents.reshape(children_here, -1)], axis=1
    )
    outgoing = jnp.dot(placer, payload, preferred_element_type=F32).astype(BF16)
    arrived = lax.all_to_all(outgoing, "search", split_axis=0, concat_axis=0, tiled=True)
    held = jnp.dot(picker, arrived, preferred_element_type=F32).astype(BF16)
    held_query = held[:, :query_cols].reshape(children_here, new_tokens, heads_here, query_width)
    held_latents = held[:, query_cols:].reshape(children_here, new_tokens, kv_width)

    latent_query = jnp.einsum(
        "cthn,hnl->cthl", held_query[..., :nope_width], up_keys, preferred_element_type=F32
    ).astype(BF16)
    full_query = jnp.concatenate([latent_query, held_query[..., nope_width:]], axis=-1)
    latent_out = attend(full_query, held_latents, parent_cache[0], latent_width, softmax_scale)
    head_out = jnp.einsum("cthl,hlv->cthv", latent_out, up_values, preferred_element_type=F32).astype(BF16)
    attention = head_out.reshape(token_rows, heads_here * value_width)

    gathered = lax.all_gather(attention, "search", axis=0, tiled=True)
    every_row = jnp.dot(gathered, out_proj, preferred_element_type=F32).astype(BF16)
    column_block = every_row.shape[1]
    every_row = jnp.take(
        every_row.reshape(children_all, new_tokens * column_block), position, axis=0
    ).reshape(children_all * new_tokens, column_block)
    owned = lax.all_to_all(every_row, "search", split_axis=0, concat_axis=1, tiled=True)
    projected = lax.psum_scatter(owned, "mp", scatter_dimension=1, tiled=True).astype(F32)
    residual = (hidden_in.reshape(token_rows, width_here).astype(F32) + projected).astype(BF16)
    residual_wide = residual.astype(F32)
    squares = jnp.sum(residual_wide * residual_wide, axis=1)
    router_part = jnp.dot(residual, router, preferred_element_type=F32)
    squares, router_part = lax.psum((squares, router_part), "mp")
    inv_rms = lax.rsqrt(squares / D + 1e-06)
    logits = router_part * inv_rms[:, None]
    normed = (residual_wide * inv_rms[:, None]).astype(BF16)

    experts_total = router.shape[1]
    picked = routes.reshape(token_rows, -1)
    affinity = jax.nn.sigmoid(logits)
    chosen_mask = jnp.any(picked[:, :, None] == jnp.arange(experts_total, dtype=I32)[None, None, :], axis=1)
    chosen = jnp.where(chosen_mask, affinity, 0.0)
    gates = 2.5 * chosen / jnp.sum(chosen, axis=1, keepdims=True)

    all_gates = lax.all_gather(gates, "search", axis=0, tiled=True)
    my_gate = jnp.sum(
        jnp.where(jnp.arange(experts_total, dtype=I32)[None, :] == me, all_gates, 0.0), axis=1
    )
    slices = lax.all_gather(normed, "search", axis=0, tiled=True)
    tokens = lax.all_gather(slices, "mp", axis=1, tiled=True)
    gate_act = jnp.dot(tokens, w_gate[0], preferred_element_type=F32)
    up_act = jnp.dot(tokens, w_up[0], preferred_element_type=F32)
    expert_hidden = (jax.nn.silu(gate_act) * up_act).astype(BF16)
    expert_part = jnp.dot(expert_hidden, w_down[0], preferred_element_type=F32)
    weighted = (expert_part * my_gate[:, None]).astype(BF16)
    weighted = lax.psum_scatter(weighted, "mp", scatter_dimension=1, tiled=True)
    expert_mix = lax.psum_scatter(weighted, "search", scatter_dimension=0, tiled=True).astype(F32)
    mixed = (residual_wide + expert_mix).astype(BF16)
    return mixed.reshape(children_here, new_tokens, width_here)


def solution(mesh):
    in_specs = (
        P("search", None, "mp", None),
        P("search", None, None),
        P("search", None, None),
        P("search"),
        P("mp", None, None),
        P("mp", None, None),
        P("mp", "search"),
        P("search", None, "mp"),
        P("mp", None),
        P("search", None, None),
        P("search", None, "mp"),
        P("search", None, "mp"),
        P("search", "mp", None),
    )
    out_specs = P("search", None, "mp")
    return jax.shard_map(local, mesh=mesh, in_specs=in_specs, out_specs=out_specs, check_vma=False)
```

time: 757 us -> 516 us (0.68); the launches traced: 742 us -> 515 us
  blocking collectives: 217 us -> 89.7 us
  matrix products: 116 us -> 44.9 us
  other arithmetic: 39.9 us -> 5.57 us
  Pallas kernels: 0 us -> 33.8 us
  local copies, waits for them, and re-layouts: 41 us -> 25 us
  starting transfers between devices: 22.3 us -> 8.69 us
    all_to_all x3 -> x1, blocking collectives: 214 us -> 18.8 us  [local(): lax.all_to_all(every_row, 'search', split_axis=0, concat_axis=1, tiled=True)]
    all_to_all x4 -> x1, waiting for transfers between devices: 135 us -> 0.01 us  [local(): lax.all_to_all(outgoing, 'search', split_axis=0, concat_axis=0, tiled=True)]
    reduce_scatter x2 -> x3, waiting for transfers between devices: 19.5 us -> 107 us  [the longest x1 89.3 us: local(): lax.psum_scatter(weighted, 'search', scatter_dimension=0, tiled=True)]
    dot_general x11 -> x8, matrix products: 111 us -> 41.4 us  [the longest x1 9.61 us: local(): gate_act = jnp.dot(tokens, w_gate[0], preferred_element_type=F32)]
    all_gather x2 -> x3, waiting for transfers between devices: 138 us -> 185 us  [the longest x1 112 us: local(): gathered = lax.all_gather(attention, 'search', axis=0, tiled=True)]
    all_gather x0 -> x1, blocking collectives: none -> 38.9 us  [local(): all_gates = lax.all_gather(gates, 'search', axis=0, tiled=True)]
    pallas_call x0 -> x1, Pallas kernels: none -> 33.8 us  [attend(): pl.pallas_call(body, grid=(tiles,), in_specs=[pl.BlockSpec((rows, kv_widt...]
    unnamed x0 -> x1, blocking collectives: none -> 29.5 us
  transfers between devices with their start and end apart: 8 -> 7, of which waited for: 7 -> 5; matrix products, arithmetic and copies ran while one was open for 5% -> 2% of each run, Pallas kernels for 0% -> 0%
where the time goes in v1:
time: 516 us; the launch traced here: 515 us
  waiting for transfers between devices  293 us (57%)
  blocking collectives  89.7 us (17%)
  matrix products  44.9 us (9%)
  Pallas kernels  33.8 us (7%)
  local copies, waits for them, and re-layouts  25 us (5%)
  between operations  14.5 us (3%)
  starting transfers between devices  8.69 us (2%)
  other arithmetic  5.57 us (1%)
    all_gather x1, waiting for transfers between devices, local(): gathered = lax.all_gather(attention, 'search', axis=0, tiled=True)  112 us
    reduce_scatter x1, waiting for transfers between devices, local(): lax.psum_scatter(weighted, 'search', scatter_dimension=0, tiled=True)  89.3 us
    all_gather x1, waiting for transfers between devices, local(): slices = lax.all_gather(normed, 'search', axis=0, tiled=True)  73.4 us
    all_gather x1, blocking collectives, local(): all_gates = lax.all_gather(gates, 'search', axis=0, tiled=True)  38.9 us
    pallas_call x1, Pallas kernels, attend(): pl.pallas_call(body, grid=(tiles,), in_specs=[pl.BlockSpec((rows, kv_widt...  33.8 us
    unnamed x1, blocking collectives  29.5 us
    all_to_all x1, blocking collectives, local(): lax.all_to_all(every_row, 'search', split_axis=0, concat_axis=1, tiled=True)  18.8 us
    reduce_scatter x1, waiting for transfers between devices, local(): weighted = lax.psum_scatter(weighted, 'mp', scatter_dimension=1, tiled=True)  11.7 us
  transfers between devices with their start and end apart: 7, of which 5 were waited for; matrix products, arithmetic and copies ran while one was open for 2% of the time, Pallas kernels for 0%

profile of v1, /device:TPU:0, one launch (start us, length us, event | category | flops | bytes accessed | tf_op | source)
XLA Modules:
  0.0 515.0 jit_solution(4011668889502995399)
XLA Ops:
  6.5 0.9 convert_reduce_fusion.2
  8.1 0.9 reshape.149
  9.0 2.5 reshape.148
  12.0 1.6 all_to_all.20
  13.6 8.4 %all-to-all-start = ((bf16[16,2,25728]{2,1,0:T(2,128)(2,1)}), bf16[16,2,25728]{2,1,0:T(2,128)(2,1)S(1)}, u32[]{:S(2)}, u32[]{:S(2)}) async-start(bf16[16,2,25728]{2,1,0:T(2,128)(2,1)} %all_to_all.20), calls=%async_computation | async-start | bytes 3293184 | tf_op jit(solution)/shard_map/all_to_all | solution.py:134
  22.1 7.7 %copy.48 = bf16[1,4096,576]{2,1,0:T(8,128)(2,1)} copy(bf16[1,4096,576]{1,2,0:T(8,128)(2,1)} %param.15) | data formatting | bytes 9437184 | tf_op args[2]
  31.3 29.5 %all-reduce = s32[256]{0:T(256)S(1)} all-reduce(s32[256]{0:T(256)S(1)} %dynamic-update-slice), channel_id=1, replica_groups=mesh['search'=16,'mp'=2] {'search'}, use_global_device_ids=true, to_apply=%add | all-reduce | flops 256 | bytes 2048
  61.3 0.7 all_to_all.22
  62.4 1.2 reshape.150
  64.3 4.8 convert_bitcast_fusion
  69.5 2.4 copy.47
  71.9 33.8 %attend.1 = bf16[2048,512]{1,0:T(8,128)(2,1)} custom-call(bf16[2048,576]{1,0:T(8,128)(2,1)} %bitcast.64, bf16[4,8,576]{2,1,0:T(8,128)(2,1)S(1)} %reshape_reshape.3.own_ref, bf16[4096,576]{1,0:T(8,128)(2,1)} %bitcast.63), custom_call_target="tpu_custom_call" | custom-call | flops 18253611008 | bytes 9175040 | tf_op jit(solution)/shard_map/attend/pallas_call | solution.py:58
  105.7 3.5 fusion.23
  109.4 1.2 copy.70
  111.0 112.1 %all-gather.5.cloned.1.call-done = bf16[512,8192]{1,0:T(8,128)(2,1)} async-done(((bf16[32,8192]{1,0:T(8,128)(2,1)}), bf16[512,8192]{1,0:T(8,128)(2,1)}) %all-gather.5.cloned.1.call-update) | async-done | bytes 8388624 | tf_op jit(solution)/shard_map/all_gather | solution.py:147
  223.1 9.4 %convolution_convert_fusion.2 = bf16[512,448]{0,1:T(8,128)(2,1)S(1)} fusion(bf16[512,8192]{1,0:T(8,128)(2,1)} %all-gather.5.cloned.1.call-done, bf16[8192,448]{0,1:T(8,128)(2,1)} %param.19), kind=kOutput, calls=%fused_computation.19 | convolution fusion | flops 3758325760 | bytes 16187392 | tf_op jit(solution)/shard_map/dot_general | solution.py:148
  233.1 1.2 gather_fusion
  234.9 18.8 %all_to_all.28 = bf16[16,32,448]{2,1,0:T(8,128)(2,1)S(1)} all-to-all(bf16[16,32,448]{2,1,0:T(8,128)(2,1)S(1)} %broadcast_select_fusion), channel_id=1, replica_groups=mesh['search'=16,'mp'=2] {'search'}, dimensions={0} | all-to-all | bytes 917504 | tf_op jit(solution)/shard_map/all_to_all | solution.py:153
  254.0 1.3 all_to_all.25
  255.5 6.2 %reduce-scatter.4.cloned.1.call-done = bf16[32,3584]{1,0:T(8,128)(2,1)} async-done(((bf16[32,7168]{1,0:T(8,128)(2,1)}), bf16[32,3584]{1,0:T(8,128)(2,1)}) %reduce-scatter.4.cloned.1.call-update) | async-done | bytes 229392 | tf_op jit(solution)/shard_map/reduce_scatter | solution.py:154
  261.7 1.1 fusion.32
  262.9 2.5 all-reduce.1
  265.4 0.8 fusion.33
  266.3 73.4 %all-gather.7.cloned.1.call-done = bf16[512,3584]{1,0:T(8,128)(2,1)} async-done(((bf16[32,3584]{1,0:T(8,128)(2,1)}), bf16[512,3584]{1,0:T(8,128)(2,1)}) %all-gather.7.cloned.1.call-update) | async-done | bytes 3670032 | tf_op jit(solution)/shard_map/all_gather | solution.py:175
  340.1 38.9 %all-gather = f32[16,32,16]{1,2,0:T(8,128)S(1)} all-gather(f32[1,32,16]{1,2,0:T(8,128)S(1)} %divide_bitcast_fusion), channel_id=1, replica_groups=mesh['search'=16,'mp'=2] {'search'}, dimensions={0}, use_global_device_ids=true | all-gather | bytes 34816 | tf_op jit(solution)/shard_map/all_gather | solution.py:171
  379.2 9.6 %fusion.7 = f32[512,512]{1,0:T(8,128)S(1)} fusion(bf16[512,7168]{1,0:T(8,128)(2,1)} %all-gather.9.cloned.1.call-done, bf16[1,7168,512]{2,1,0:T(8,128)(2,1)} %param.23), kind=kOutput, calls=%fused_computation.11 | convolution fusion | flops 3758096384 | bytes 15728640 | tf_op jit(solution)/shard_map/dot_general | solution.py:177
  388.8 7.2 %fusion.15 = bf16[512,512]{1,0:T(8,128)(2,1)S(1)} fusion(bf16[512,7168]{1,0:T(8,128)(2,1)S(1)} %copy-done.3, bf16[1,7168,512]{2,1,0:T(8,128)(2,1)} %param.24, f32[512,512]{1,0:T(8,128)S(1)} %fusion.7), kind=kOutput, calls=%fused_computation.17 | convolution fusion | flops 3759669248 | bytes 16252928 | tf_op jit(solution)/shard_map/dot_general | solution.py:178
  396.0 9.2 %multiply_convert_fusion = bf16[512,7168]{1,0:T(8,128)(2,1)} fusion(bf16[512,512]{1,0:T(8,128)(2,1)S(1)} %fusion.15, bf16[1,512,7168]{2,1,0:T(8,128)(2,1)} %param.25, f32[512]{0:T(512)S(1)} %select_reduce_fusion), kind=kOutput, calls=%fused_computation.3 | convolution fusion | flops 3765436416 | bytes 15206400 | tf_op jit(solution)/shard_map/dot_general | solution.py:180
  405.3 11.7 %reduce-scatter.6.cloned.1.call-done = bf16[512,3584]{1,0:T(8,128)(2,1)} async-done(((bf16[512,7168]{1,0:T(8,128)(2,1)}), bf16[512,3584]{1,0:T(8,128)(2,1)}) %reduce-scatter.6.cloned.1.call-update) | async-done | bytes 3670032 | tf_op jit(solution)/shard_map/reduce_scatter | solution.py:182
  417.1 89.3 %reduce-scatter.8.cloned.1.call-done = bf16[32,3584]{1,0:T(8,128)(2,1)} async-done(((bf16[512,3584]{1,0:T(8,128)(2,1)}), bf16[32,3584]{1,0:T(8,128)(2,1)}) %reduce-scatter.8.cloned.1.call-update) | async-done | bytes 229392 | tf_op jit(solution)/shard_map/reduce_scatter | solution.py:183
  506.4 1.0 fusion.34
  507.4 0.8 reshape.155
  (75 shorter events, 6.9 us)
Async XLA Ops:
  6.5 256.2 %copy-start = (bf16[3584,16]{0,1:T(8,128)(2,1)S(1)}, bf16[3584,16]{0,1:T(8,128)(2,1)}, u32[]{:S(2)}) copy-start(bf16[3584,16]{0,1:T(8,128)(2,1)} %param.21) | copy-start | bytes 344068
  13.6 16.2 %copy-start.5 = (u32[32]{0:T(128)S(1)}, u32[32]{0:T(128)}, u32[]{:S(2)}) copy-start(u32[32]{0:T(128)} %constant.88) | copy-start | bytes 388
  13.6 17.4 %copy-start.4 = (s32[16]{0:T(128)S(1)}, s32[16]{0:T(128)}, u32[]{:S(2)}) copy-start(s32[16]{0:T(128)} %param.16) | copy-start | bytes 196
  13.6 47.6 %all-to-all-start = ((bf16[16,2,25728]{2,1,0:T(2,128)(2,1)}), bf16[16,2,25728]{2,1,0:T(2,128)(2,1)S(1)}, u32[]{:S(2)}, u32[]{:S(2)}) async-start(bf16[16,2,25728]{2,1,0:T(2,128)(2,1)} %all_to_all.20), calls=%async_computation | async-start | bytes 3293184 | tf_op jit(solution)/shard_map/all_to_all | solution.py:134
  22.1 201.0 %all-gather.5.cloned.1.call-start = ((), (), s32[]{:S(2)}) async-start(), calls=%async_computation.5 | async-start | bytes 8912896 | tf_op jit(solution)/shard_map/all_gather | solution.py:147
  69.4 36.3 %slice-start = ((s8[8388608]{0:T(1024)(128)(4,1)}), s8[4194304]{0:T(1024)(128)(4,1)S(1)}, s32[]{:S(2)}) async-start(s8[8388608]{0:T(1024)(128)(4,1)} %bitcast.60), calls=%async_computation.11 | async-start | bytes 8388608
  71.9 33.8 %slice-start.1 = ((s8[8388608]{0:T(1024)(128)(4,1)}), s8[4194304]{0:T(1024)(128)(4,1)S(1)}, s32[]{:S(2)}) async-start(s8[8388608]{0:T(1024)(128)(4,1)} %bitcast.60), calls=%async_computation.12 | async-start | bytes 8388608
  110.7 151.0 %reduce-scatter.4.cloned.1.call-start = ((), (), s32[]{:S(2)}) async-start(), calls=%async_computation.6 | async-start | bytes 688128 | tf_op jit(solution)/shard_map/reduce_scatter | solution.py:154
  232.5 22.8 %copy-start.1 = (bf16[16,2,3584]{2,1,0:T(2,128)(2,1)S(1)}, bf16[16,2,3584]{2,1,0:T(2,128)(2,1)}, u32[]{:S(2)}) copy-start(bf16[16,2,3584]{2,1,0:T(2,128)(2,1)} %param.20) | copy-start | bytes 688132
  233.1 106.7 %copy-start.2 = (s32[16,2,8]{0,2,1:T(8,128)S(1)}, s32[16,2,8]{0,2,1:T(8,128)}, u32[]{:S(2)}) copy-start(s32[16,2,8]{0,2,1:T(8,128)} %param.22) | copy-start | bytes 3076
  255.3 84.4 %all-gather.7.cloned.1.call-start = ((), (), s32[]{:S(2)}) async-start(), calls=%async_computation.7 | async-start | bytes 3899392 | tf_op jit(solution)/shard_map/all_gather | solution.py:175
  266.3 112.9 %all-gather.9.cloned.1.call-start = ((), (), s32[]{:S(2)}) async-start(), calls=%async_computation.8 | async-start | bytes 11010048 | tf_op jit(solution)/shard_map/all_gather | solution.py:176
  339.8 77.3 %reduce-scatter.6.cloned.1.call-start = ((), (), s32[]{:S(2)}) async-start(), calls=%async_computation.9 | async-start | bytes 11010048 | tf_op jit(solution)/shard_map/reduce_scatter | solution.py:182
  379.2 9.6 %copy-start.3 = (bf16[512,7168]{1,0:T(8,128)(2,1)S(1)}, bf16[512,7168]{1,0:T(8,128)(2,1)}, u32[]{:S(2)}) copy-start(bf16[512,7168]{1,0:T(8,128)(2,1)} %all-gather.9.cloned.1.call-done) | copy-start | bytes 22020100
  405.3 101.1 %reduce-scatter.8.cloned.1.call-start = ((), (), s32[]{:S(2)}) async-start(), calls=%async_computation.10 | async-start | bytes 3899392 | tf_op jit(solution)/shard_map/reduce_scatter | solution.py:183
Sparse Core Ops, SparseCore 0:
  110.8 112.2 all-gather.4
  255.5 6.1 reduce-scatter.3
  266.4 73.2 all-gather.6
  341.2 16.8 all-gather.8
  405.4 11.6 reduce-scatter.5
  419.2 87.1 reduce-scatter.7

commit v2 on v1

--- a/solution.py
+++ b/solution.py
@@ -77,6 +77,190 @@
     return out.reshape(children, steps, heads, latent_width)
 
 
+def gather_kernel(across, x_ref, o_ref, send_sem, recv_sem, core_send, core_recv, local_sem):
+    me, core = lax.axis_index("search"), lax.axis_index("mp")
+    x, y, z = lax.rem(me, 2), lax.rem(lax.div(me, 2), 2), lax.div(me, 4)
+    half = x_ref.shape[0] // 2
+
+    def at(zz, yy, xx):
+        return (zz * 2 + yy) * 2 + xx
+
+    x_peer, y_peer, above, below = at(z, y, 1 - x), at(z, 1 - y, x), me + 4, me - 4
+    has_above, has_below = z < 3, z > 0
+
+    def block(item):
+        return o_ref.at[core, item] if across else o_ref.at[item]
+
+    def remote(src, dst, sent, landed, device):
+        return pltpu.make_async_remote_copy(
+            src_ref=src, dst_ref=dst, send_sem=sent, recv_sem=landed,
+            device_id=device, device_id_type=pl.DeviceIdType.MESH,
+        )
+
+    def send(kind, landing, zc, item, target, src=None, rows=None):
+        dst = block(item) if rows is None else block(item).at[rows]
+        return remote(dst if src is None else src, dst, send_sem.at[kind, zc], recv_sem.at[landing, zc],
+                      (target, core))
+
+    def to_core(item, src=None):
+        return remote(block(item) if src is None else src, block(item), core_send.at[item], core_recv.at[item],
+                      (me, 1 - core))
+
+    def share(item, src=None):
+        if across:
+            to_core(item, src).start()
+
+    low, high = pl.ds(0, half), pl.ds(half, half)
+    barrier = pltpu.get_barrier_semaphore()
+
+    def greet(device):
+        pl.semaphore_signal(barrier, inc=1, device_id=device, device_id_type=pl.DeviceIdType.MESH)
+
+    greet((x_peer, core))
+    greet((y_peer, core))
+    if across:
+        greet((me, 1 - core))
+
+    @pl.when(has_above)
+    def _():
+        greet((above, core))
+
+    @pl.when(has_below)
+    def _():
+        greet((below, core))
+
+    pl.semaphore_wait(barrier, (4 if across else 3) + lax.div(z * (3 - z), 2))
+
+    def spread(zc, src=None):
+        item = at(zc, y, x)
+        send(2, 1, zc, item, x_peer, src).start()
+        send(3, 2, zc, item, y_peer, src).start()
+
+    def climb(zc, src=None):
+        @pl.when(has_above)
+        def _():
+            send(0, 0, zc, at(zc, y, x), above, src).start()
+
+    def descend(zc, src=None):
+        @pl.when(has_below)
+        def _():
+            send(1, 0, zc, at(zc, y, x), below, src).start()
+
+    def relay(zc):
+        from_x, from_y = at(zc, y, 1 - x), at(zc, 1 - y, x)
+        send(2, 1, zc, from_x, x_peer).wait_recv()
+        send(5, 4, zc, from_x, y_peer, rows=low).start()
+        send(3, 2, zc, from_y, y_peer).wait_recv()
+        send(4, 3, zc, from_y, x_peer, rows=high).start()
+        share(from_x)
+        share(from_y)
+
+    climb(z, x_ref)
+    descend(z, x_ref)
+    spread(z, x_ref)
+    share(me, x_ref)
+    own = pltpu.make_async_copy(x_ref, block(me), local_sem)
+    own.start()
+    for k in range(1, 4):
+        @pl.when(z >= k)
+        def _():
+            zc = z - k
+            send(0, 0, zc, at(zc, y, x), above).wait_recv()
+            climb(zc)
+            spread(zc)
+            share(at(zc, y, x))
+
+        @pl.when(z + k < 4)
+        def _():
+            zc = z + k
+            send(0, 0, zc, at(zc, y, x), above).wait_recv()
+            descend(zc)
+            spread(zc)
+            share(at(zc, y, x))
+
+        if k == 1:
+            relay(z)
+        else:
+            @pl.when(z >= k - 1)
+            def _():
+                relay(z - (k - 1))
+
+            @pl.when(z + k - 1 < 4)
+            def _():
+                relay(z + (k - 1))
+
+    @pl.when(z >= 3)
+    def _():
+        relay(z - 3)
+
+    @pl.when(z + 3 < 4)
+    def _():
+        relay(z + 3)
+
+    for zc in range(4):
+        diagonal = at(zc, 1 - y, 1 - x)
+        send(5, 4, zc, diagonal, y_peer, rows=low).wait_recv()
+        send(4, 3, zc, diagonal, x_peer, rows=high).wait_recv()
+        share(diagonal)
+    for zc in range(4):
+        @pl.when((z >= zc) & has_above)
+        def _():
+            send(0, 0, zc, at(zc, y, x), above).wait_send()
+
+        @pl.when((z <= zc) & has_below)
+        def _():
+            send(1, 0, zc, at(zc, y, x), below).wait_send()
+
+        send(2, 1, zc, at(zc, y, x), x_peer).wait_send()
+        send(3, 2, zc, at(zc, y, x), y_peer).wait_send()
+        send(4, 3, zc, at(zc, 1 - y, x), x_peer, rows=high).wait_send()
+        send(5, 4, zc, at(zc, y, 1 - x), y_peer, rows=low).wait_send()
+    own.wait()
+    if across:
+        for item in range(16):
+            to_core(item).wait_send()
+            remote(o_ref.at[1 - core, item], o_ref.at[1 - core, item], core_send.at[item], core_recv.at[item],
+                   (me, 1 - core)).wait_recv()
+
+
+def gather_blocks(block, across, collective_id):
+    shape = ((2, 16) if across else (16,)) + block.shape
+    return pl.pallas_call(
+        functools.partial(gather_kernel, across),
+        out_shape=jax.ShapeDtypeStruct(shape, block.dtype),
+        in_specs=[pl.BlockSpec(memory_space=pl.ANY)],
+        out_specs=pl.BlockSpec(memory_space=pl.ANY),
+        scratch_shapes=[
+            pltpu.SemaphoreType.DMA((6, 4)),
+            pltpu.SemaphoreType.DMA((5, 4)),
+            pltpu.SemaphoreType.DMA((16,)),
+            pltpu.SemaphoreType.DMA((16,)),
+            pltpu.SemaphoreType.DMA,
+        ],
+        compiler_params=pltpu.CompilerParams(collective_id=collective_id, has_side_effects=True),
+        name="gather_tokens" if across else "gather_heads",
+    )(block)
+
+
+def fold(values, axis, distance):
+    count = lax.axis_size("search")
+    bit = lax.rem(lax.div(lax.axis_index("search"), distance), 2)
+    keep = lax.dynamic_index_in_dim(values, bit, axis, keepdims=False)
+    give = lax.dynamic_index_in_dim(values, 1 - bit, axis, keepdims=False)
+    got = lax.ppermute(give, "search", [(i, i ^ distance) for i in range(count)])
+    return (keep.astype(F32) + got.astype(F32)).astype(values.dtype)
+
+
+def scatter_sum(values, rows):
+    width = values.shape[1]
+    split = values.reshape(2, 2, 2, 2, rows, width)
+    first, second = split[..., : width // 2], split[..., width // 2:]
+    first = fold(fold(first, 3, 1), 2, 2)
+    second = fold(fold(second, 2, 2), 2, 1)
+    both = jnp.concatenate([first, second], axis=-1)
+    return fold(fold(both, 1, 4), 0, 8)
+
+
 def local(
     queries,
     new_latents,
@@ -144,7 +328,11 @@
     head_out = jnp.einsum("cthl,hlv->cthv", latent_out, up_values, preferred_element_type=F32).astype(BF16)
     attention = head_out.reshape(token_rows, heads_here * value_width)
 
-    gathered = lax.all_gather(attention, "search", axis=0, tiled=True)
+    block_4x2x2 = searchers == 16 and lax.axis_size("mp") == 2
+    if block_4x2x2:
+        gathered = gather_blocks(attention, False, 0).reshape(searchers * token_rows, -1)
+    else:
+        gathered = lax.all_gather(attention, "search", axis=0, tiled=True)
     every_row = jnp.dot(gathered, out_proj, preferred_element_type=F32).astype(BF16)
     column_block = every_row.shape[1]
     every_row = jnp.take(
@@ -168,19 +356,35 @@
     chosen = jnp.where(chosen_mask, affinity, 0.0)
     gates = 2.5 * chosen / jnp.sum(chosen, axis=1, keepdims=True)
 
-    all_gates = lax.all_gather(gates, "search", axis=0, tiled=True)
+    if block_4x2x2:
+        gates_high = gates.astype(BF16)
+        gates_low = (gates - gates_high.astype(F32)).astype(BF16)
+        spare = jnp.zeros((token_rows, 128 - 2 * experts_total), BF16)
+        block = jnp.concatenate([normed, gates_high, gates_low, spare], axis=1)
+        slices = gather_blocks(block, True, 1).reshape(2, searchers * token_rows, width_here + 128)
+        sent = slices[0, :, width_here:].astype(F32)
+        all_gates = sent[:, :experts_total] + sent[:, experts_total : 2 * experts_total]
+        slices = [slices[part, :, :width_here] for part in range(2)]
+    else:
+        all_gates = lax.all_gather(gates, "search", axis=0, tiled=True)
+        slices = lax.all_gather(normed, "search", axis=0, tiled=True)
+        slices = lax.all_gather(slices, "mp", axis=0)
     my_gate = jnp.sum(
         jnp.where(jnp.arange(experts_total, dtype=I32)[None, :] == me, all_gates, 0.0), axis=1
     )
-    slices = lax.all_gather(normed, "search", axis=0, tiled=True)
-    tokens = lax.all_gather(slices, "mp", axis=1, tiled=True)
-    gate_act = jnp.dot(tokens, w_gate[0], preferred_element_type=F32)
-    up_act = jnp.dot(tokens, w_up[0], preferred_element_type=F32)
+    gate_act, up_act = 0.0, 0.0
+    for part in range(len(slices)):
+        span = slice(part * width_here, (part + 1) * width_here)
+        gate_act += jnp.dot(slices[part], w_gate[0, span], preferred_element_type=F32)
+        up_act += jnp.dot(slices[part], w_up[0, span], preferred_element_type=F32)
     expert_hidden = (jax.nn.silu(gate_act) * up_act).astype(BF16)
     expert_part = jnp.dot(expert_hidden, w_down[0], preferred_element_type=F32)
     weighted = (expert_part * my_gate[:, None]).astype(BF16)
     weighted = lax.psum_scatter(weighted, "mp", scatter_dimension=1, tiled=True)
-    expert_mix = lax.psum_scatter(weighted, "search", scatter_dimension=0, tiled=True).astype(F32)
+    if block_4x2x2:
+        expert_mix = scatter_sum(weighted, token_rows).astype(F32)
+    else:
+        expert_mix = lax.psum_scatter(weighted, "search", scatter_dimension=0, tiled=True).astype(F32)
     mixed = (residual_wide + expert_mix).astype(BF16)
     return mixed.reshape(children_here, new_tokens, width_here)
 

time: 516 us -> 379 us (0.73)
  waiting for transfers between devices: 293 us -> 68.6 us
  Pallas kernels: 33.8 us -> 145 us
  blocking collectives: 89.7 us -> 49.9 us
  starting transfers between devices: 8.69 us -> 18.2 us
  local copies, waits for them, and re-layouts: 25 us -> 32.4 us
    all_gather x3 -> x0, waiting for transfers between devices: 185 us -> none  [the longest x1 112 us: local(): gathered = lax.all_gather(attention, 'search', axis=0, tiled=True)]
    pallas_call x0 -> x2, Pallas kernels: none -> 111 us  [gather_blocks(): pl.pallas_call(functools.partial(gather_kernel, across), out_shape=jax.Sh...]
    reduce_scatter x1 -> x0, waiting for transfers between devices: 89.3 us -> none  [local(): lax.psum_scatter(weighted, 'search', scatter_dimension=0, tiled=True)]
    ppermute x0 -> x6, waiting for transfers between devices: none -> 46.5 us  [fold(): lax.ppermute(give, 'search', [(i, i ^ distance) for i in range(count)])]
    all_gather x1 -> x0, blocking collectives: 38.9 us -> none  [local(): all_gates = lax.all_gather(gates, 'search', axis=0, tiled=True)]
    ppermute x0 -> x6, starting transfers between devices: none -> 9.84 us  [fold(): lax.ppermute(give, 'search', [(i, i ^ distance) for i in range(count)])]
    unnamed x24 -> x35, local copies, waits for them, and re-layouts: 10.2 us -> 13.2 us
    dot_general x2 -> x4, matrix products: 16.8 us -> 13.9 us  [the longest x2 9.69 us: local(): jnp.dot(slices[part], w_gate[0, span], preferred_element_type=F32)]
  transfers between devices with their start and end apart: 7 -> 9, of which waited for: 5 -> 8; matrix products, arithmetic and copies ran while one was open for 2% -> 4% of each run, Pallas kernels for 0% -> 0%
where the time goes in v2:
time: 379 us
  Pallas kernels  145 us (38%)
  waiting for transfers between devices  68.6 us (18%)
  blocking collectives  49.9 us (13%)
  matrix products  41.3 us (11%)
  local copies, waits for them, and re-layouts  32.4 us (9%)
  starting transfers between devices  18.2 us (5%)
  between operations  14.6 us (4%)
  other arithmetic  8.61 us (2%)
    pallas_call x2, Pallas kernels, gather_blocks(): pl.pallas_call(functools.partial(gather_kernel, across), out_shape=jax.Sh...  111 us
    ppermute x6, waiting for transfers between devices, fold(): lax.ppermute(give, 'search', [(i, i ^ distance) for i in range(count)])  46.5 us
    pallas_call x1, Pallas kernels, attend(): pl.pallas_call(body, grid=(tiles,), in_specs=[pl.BlockSpec((rows, kv_widt...  33.7 us
    unnamed x1, blocking collectives  29.5 us
    all_to_all x1, blocking collectives, local(): lax.all_to_all(every_row, 'search', split_axis=0, concat_axis=1, tiled=True)  17 us
    reduce_scatter x1, waiting for transfers between devices, local(): weighted = lax.psum_scatter(weighted, 'mp', scatter_dimension=1, tiled=True)  16.2 us
    unnamed x35, local copies, waits for them, and re-layouts  13.2 us
    ppermute x6, starting transfers between devices, fold(): lax.ppermute(give, 'search', [(i, i ^ distance) for i in range(count)])  9.84 us
  transfers between devices with their start and end apart: 9, of which 8 were waited for; matrix products, arithmetic and copies ran while one was open for 4% of the time, Pallas kernels for 0%

profile of v2, /device:TPU:0, one launch (start us, length us, event | category | flops | bytes accessed | tf_op | source)
XLA Modules:
  0.0 378.7 jit_solution(3101468187463458484)
XLA Ops:
  6.5 2.5 reshape.171
  12.1 1.6 all_to_all.20
  13.6 8.3 %all-to-all-start = ((bf16[16,2,25728]{2,1,0:T(2,128)(2,1)}), bf16[16,2,25728]{2,1,0:T(2,128)(2,1)S(1)}, u32[]{:S(2)}, u32[]{:S(2)}) async-start(bf16[16,2,25728]{2,1,0:T(2,128)(2,1)} %all_to_all.20), calls=%async_computation | async-start | bytes 3293184 | tf_op jit(solution)/shard_map/all_to_all | solution.py:318
  22.0 7.6 %copy.54 = bf16[1,4096,576]{2,1,0:T(8,128)(2,1)} copy(bf16[1,4096,576]{1,2,0:T(8,128)(2,1)} %param.15) | data formatting | bytes 9437184 | tf_op args[2]
  31.2 29.5 %all-reduce = s32[256]{0:T(256)S(1)} all-reduce(s32[256]{0:T(256)S(1)} %dynamic-update-slice), channel_id=1, replica_groups=mesh['search'=16,'mp'=2] {'search'}, use_global_device_ids=true, to_apply=%add | all-reduce | flops 256 | bytes 2048
  65.4 4.8 %convert_bitcast_fusion = bf16[16,2,64,512]{3,0,1,2:T(8,128)(2,1)S(1)} fusion(bf16[64,128,512]{2,1,0:T(8,128)(2,1)} %param.17, bf16[16,2,64,128]{3,2,1,0:T(8,128)(2,1)S(1)} %slice.63), kind=kOutput, calls=%fused_computation.25 | convolution fusion | flops 269484032 | bytes 11010048 | tf_op jit(solution)/shard_map/cthn,hnl->cthl/dot_general | solution.py:323
  70.6 2.4 copy.53
  73.1 33.7 %attend.1 = bf16[2048,512]{1,0:T(8,128)(2,1)} custom-call(bf16[2048,576]{1,0:T(8,128)(2,1)} %bitcast.137, bf16[4,8,576]{2,1,0:T(8,128)(2,1)S(1)} %reshape_reshape.3.own_ref, bf16[4096,576]{1,0:T(8,128)(2,1)} %bitcast.135), custom_call_target="tpu_custom_call" | custom-call | flops 18253611008 | bytes 9175040 | tf_op jit(solution)/shard_map/attend/pallas_call | solution.py:58
  106.7 5.9 %fusion.39 = bf16[16,2,64,128]{3,0,1,2:T(8,128)(2,1)S(1)} fusion(bf16[64,512,128]{2,1,0:T(8,128)(2,1)} %param.18, bf16[16,2,64,512]{3,2,1,0:T(8,128)(2,1)} %bitcast.134), kind=kOutput, calls=%fused_computation.36 | convolution fusion | flops 268697600 | bytes 11010048 | tf_op jit(solution)/shard_map/cthl,hlv->cthv/dot_general | solution.py:328
  114.1 71.4 %gather_heads.1 = bf16[16,32,8192]{2,1,0:T(8,128)(2,1)} custom-call(bf16[32,8192]{1,0:T(8,128)(2,1)} %bitcast.138), custom_call_target="tpu_custom_call" | custom-call | tf_op jit(solution)/shard_map/gather_heads/pallas_call | solution.py:228
  185.5 9.4 %convolution_convert_fusion.2 = bf16[512,448]{0,1:T(8,128)(2,1)S(1)} fusion(bf16[512,8192]{1,0:T(8,128)(2,1)} %bitcast.126, bf16[8192,448]{0,1:T(8,128)(2,1)} %param.19), kind=kOutput, calls=%fused_computation.35 | convolution fusion | flops 3758325760 | bytes 16187392 | tf_op jit(solution)/shard_map/dot_general | solution.py:336
  197.3 17.0 %all_to_all.28 = bf16[16,32,448]{2,1,0:T(8,128)(2,1)S(1)} all-to-all(bf16[16,32,448]{2,1,0:T(8,128)(2,1)S(1)} %broadcast_select_fusion), channel_id=1, replica_groups=mesh['search'=16,'mp'=2] {'search'}, dimensions={0} | all-to-all | bytes 917504 | tf_op jit(solution)/shard_map/all_to_all | solution.py:341
  216.3 5.8 %reduce-scatter.3.cloned.1.call-done = bf16[32,3584]{1,0:T(8,128)(2,1)} async-done(((bf16[32,7168]{1,0:T(8,128)(2,1)}), bf16[32,3584]{1,0:T(8,128)(2,1)}) %reduce-scatter.3.cloned.1.call-update) | async-done | bytes 229392 | tf_op jit(solution)/shard_map/reduce_scatter | solution.py:342
  223.5 3.4 all-reduce.1
  228.1 39.9 %gather_tokens.1 = bf16[2,16,32,3712]{3,2,1,0:T(8,128)(2,1)} custom-call(bf16[32,3712]{1,0:T(8,128)(2,1)} %concatenate.14.x_ref), custom_call_target="tpu_custom_call" | custom-call | tf_op jit(solution)/shard_map/gather_tokens/pallas_call | solution.py:228
  269.1 5.4 %fusion.9 = f32[512,512]{1,0:T(8,128)S(1)} fusion(bf16[1,7168,512]{2,1,0:T(8,128)(2,1)} %param.23, bf16[2,512,3712]{2,1,0:T(8,128)(2,1)} %bitcast.128), kind=kOutput, calls=%fused_computation.15 | convolution fusion | flops 1879048192 | bytes 8388608 | tf_op jit(solution)/shard_map/dot_general | solution.py:378
  274.6 4.2 %fusion.22 = f32[512,512]{1,0:T(8,128)S(1)} fusion(f32[512,512]{1,0:T(8,128)S(1)} %fusion.9, bf16[1,7168,512]{2,1,0:T(8,128)(2,1)} %param.23, bf16[2,512,3712]{2,1,0:T(8,128)(2,1)S(1)} %bitcast.131), kind=kOutput, calls=%fused_computation.30 | convolution fusion | flops 1879310336 | bytes 9437184 | tf_op jit(solution)/shard_map/dot_general | solution.py:378
  278.8 2.1 fusion.5
  280.9 2.2 fusion.31
  283.4 6.0 %multiply_convert_fusion = bf16[512,7168]{1,0:T(8,128)(2,1)} fusion(bf16[512,512]{1,0:T(8,128)(2,1)S(1)} %fusion.31, bf16[1,512,7168]{2,1,0:T(8,128)(2,1)S(1)} %bitcast.145, f32[512]{0:T(512)S(1)} %fusion.60), kind=kOutput, calls=%fused_computation.3 | convolution fusion | flops 3765436416 | bytes 15206400 | tf_op jit(solution)/shard_map/dot_general | solution.py:381
  289.4 16.2 %reduce-scatter.5.cloned.1.call-done = bf16[512,3584]{1,0:T(8,128)(2,1)} async-done(((bf16[512,7168]{1,0:T(8,128)(2,1)}), bf16[512,3584]{1,0:T(8,128)(2,1)}) %reduce-scatter.5.cloned.1.call-update) | async-done | bytes 3670032 | tf_op jit(solution)/shard_map/reduce_scatter | solution.py:383
  305.7 2.4 fusion.70
  309.3 1.6 collective-permute-start.2
  312.9 1.6 collective-permute-start
  314.5 17.6 %collective-permute-done.2 = bf16[2,2,2,32,1792]{4,3,0,1,2:T(8,128)(2,1)} collective-permute-done((bf16[2,2,2,32,1792]{4,3,0,1,2:T(8,128)(2,1)}, bf16[2,2,2,32,1792]{4,3,0,1,2:T(8,128)(2,1)}, u32[]{:S(2)}, u32[]{:S(2)}) %collective-permute-start.2) | collective-permute-done | bytes 917536 | tf_op jit(solution)/shard_map/ppermute | solution.py:250
  333.6 1.7 collective-permute-start.3
  338.4 7.1 %collective-permute-done.3 = bf16[2,2,32,1792]{3,2,0,1:T(8,128)(2,1)S(1)} collective-permute-done((bf16[2,2,32,1792]{3,2,0,1:T(8,128)(2,1)S(1)}, bf16[2,2,32,1792]{3,2,0,1:T(8,128)(2,1)S(1)}, u32[]{:S(2)}, u32[]{:S(2)}) %collective-permute-start.3) | collective-permute-done | bytes 458784 | tf_op jit(solution)/shard_map/ppermute | solution.py:250
  345.7 3.3 collective-permute-done.1
  349.1 1.5 collective-permute-start.4
  350.6 9.4 %collective-permute-done.4 = bf16[2,32,3584]{2,1,0:T(8,128)(2,1)S(1)} collective-permute-done((bf16[2,32,3584]{2,1,0:T(8,128)(2,1)S(1)}, bf16[2,32,3584]{2,1,0:T(8,128)(2,1)S(1)}, u32[]{:S(2)}, u32[]{:S(2)}) %collective-permute-start.4) | collective-permute-done | bytes 458784 | tf_op jit(solution)/shard_map/ppermute | solution.py:250
  360.2 2.3 collective-permute-start.5
  362.4 8.6 %collective-permute-done.5 = bf16[32,3584]{1,0:T(8,128)(2,1)S(1)} collective-permute-done((bf16[32,3584]{1,0:T(8,128)(2,1)S(1)}, bf16[32,3584]{1,0:T(8,128)(2,1)S(1)}, u32[]{:S(2)}, u32[]{:S(2)}) %collective-permute-start.5) | collective-permute-done | bytes 229408 | tf_op jit(solution)/shard_map/ppermute | solution.py:250
  (107 shorter events, 27.5 us)
Async XLA Ops:
  6.5 216.8 %copy-start = (bf16[3584,16]{0,1:T(8,128)(2,1)S(1)}, bf16[3584,16]{0,1:T(8,128)(2,1)}, u32[]{:S(2)}) copy-start(bf16[3584,16]{0,1:T(8,128)(2,1)} %param.21) | copy-start | bytes 344068
  13.6 47.8 %all-to-all-start = ((bf16[16,2,25728]{2,1,0:T(2,128)(2,1)}), bf16[16,2,25728]{2,1,0:T(2,128)(2,1)S(1)}, u32[]{:S(2)}, u32[]{:S(2)}) async-start(bf16[16,2,25728]{2,1,0:T(2,128)(2,1)} %all_to_all.20), calls=%async_computation | async-start | bytes 3293184 | tf_op jit(solution)/shard_map/all_to_all | solution.py:318
  22.0 200.2 %reduce-scatter.3.cloned.1.call-start = ((), (), s32[]{:S(2)}) async-start(), calls=%async_computation.4 | async-start | bytes 688128 | tf_op jit(solution)/shard_map/reduce_scatter | solution.py:342
  22.0 7.7 %copy-start.6 = (u32[32]{0:T(128)S(1)}, u32[32]{0:T(128)}, u32[]{:S(2)}) copy-start(u32[32]{0:T(128)} %constant.147) | copy-start | bytes 388
  22.0 8.9 %copy-start.5 = (s32[16]{0:T(128)S(1)}, s32[16]{0:T(128)}, u32[]{:S(2)}) copy-start(s32[16]{0:T(128)} %param.16) | copy-start | bytes 196
  62.6 1.0 copy-start.2
  70.5 2.4 slice-start.2
  196.7 19.2 %copy-start.3 = (bf16[16,2,3584]{2,1,0:T(2,128)(2,1)S(1)}, bf16[16,2,3584]{2,1,0:T(2,128)(2,1)}, u32[]{:S(2)}) copy-start(bf16[16,2,3584]{2,1,0:T(2,128)(2,1)} %param.20) | copy-start | bytes 688132
  196.7 19.3 %copy-start.4 = (s32[16,2,8]{0,2,1:T(8,128)S(1)}, s32[16,2,8]{0,2,1:T(8,128)}, u32[]{:S(2)}) copy-start(s32[16,2,8]{0,2,1:T(8,128)} %param.22) | copy-start | bytes 3076
  215.9 89.8 %reduce-scatter.5.cloned.1.call-start = ((), (), s32[]{:S(2)}) async-start(), calls=%async_computation.5 | async-start | bytes 11010048 | tf_op jit(solution)/shard_map/reduce_scatter | solution.py:383
  267.9 6.6 %slice-start = ((s8[7602176]{0:T(1024)(128)(4,1)}), s8[4194304]{0:T(1024)(128)(4,1)S(1)}, s32[]{:S(2)}) async-start(s8[7602176]{0:T(1024)(128)(4,1)} %bitcast.129), calls=%async_computation.6 | async-start | bytes 8388608
  269.0 5.5 %slice-start.1 = ((s8[7602176]{0:T(1024)(128)(4,1)}), s8[3407872]{0:T(1024)(128)(4,1)S(1)}, s32[]{:S(2)}) async-start(s8[7602176]{0:T(1024)(128)(4,1)} %bitcast.129), calls=%async_computation.7 | async-start | bytes 6815744
  269.0 9.8 %slice-start.3 = ((s8[7340032]{0:T(1024)(128)(4,1)}), s8[4194304]{0:T(1024)(128)(4,1)S(1)}, s32[]{:S(2)}) async-start(s8[7340032]{0:T(1024)(128)(4,1)} %bitcast.142), calls=%async_computation.9 | async-start | bytes 8388608
  274.5 4.3 %slice-start.4 = ((s8[7340032]{0:T(1024)(128)(4,1)}), s8[3145728]{0:T(1024)(128)(4,1)S(1)}, s32[]{:S(2)}) async-start(s8[7340032]{0:T(1024)(128)(4,1)} %bitcast.142), calls=%async_computation.10 | async-start | bytes 6291456
  278.8 4.5 %slice-start.5 = ((s8[7340032]{0:T(1024)(128)(4,1)}), s8[4194304]{0:T(1024)(128)(4,1)S(1)}, s32[]{:S(2)}) async-start(s8[7340032]{0:T(1024)(128)(4,1)} %bitcast.144), calls=%async_computation.11 | async-start | bytes 8388608
  280.9 2.4 slice-start.6
  309.3 22.9 %collective-permute-start.2 = (bf16[2,2,2,32,1792]{4,3,0,1,2:T(8,128)(2,1)}, bf16[2,2,2,32,1792]{4,3,0,1,2:T(8,128)(2,1)}, u32[]{:S(2)}, u32[]{:S(2)}) collective-permute-start(bf16[2,2,2,32,1792]{4,3,0,1,2:T(8,128)(2,1)} %bitcast.123), channel_id=1, source_target_pairs={{0,4},{2,6},{4,0},{6,2},{8,12},{10,14},{12,8},{14,10},{16,20},{18,... | collective-permute-start | bytes 2752520 | tf_op jit(solution)/shard_map/ppermute | solution.py:250
  312.9 22.7 %collective-permute-start = (bf16[2,2,2,32,1792]{4,3,0,1,2:T(8,128)(2,1)}, bf16[2,2,2,32,1792]{4,3,0,1,2:T(8,128)(2,1)}, u32[]{:S(2)}, u32[]{:S(2)}) collective-permute-start(bf16[2,2,2,32,1792]{4,3,0,1,2:T(8,128)(2,1)} %bitcast.124), channel_id=1, source_target_pairs={{0,2},{2,0},{4,6},{6,4},{8,10},{10,8},{12,14},{14,12},{16,18},{18,... | collective-permute-start | bytes 2752520 | tf_op jit(solution)/shard_map/ppermute | solution.py:250
  314.5 21.2 %copy-start.1 = (bf16[2,2,2,1,32,1792]{5,4,3,2,1,0:T(8,128)(2,1)S(1)}, bf16[2,2,2,1,32,1792]{5,4,3,2,1,0:T(8,128)(2,1)}, u32[]{:S(2)}) copy-start(bf16[2,2,2,1,32,1792]{5,4,3,2,1,0:T(8,128)(2,1)} %get-tuple-element.19) | copy-start | bytes 2752516
  333.6 12.0 %collective-permute-start.3 = (bf16[2,2,32,1792]{3,2,0,1:T(8,128)(2,1)S(1)}, bf16[2,2,32,1792]{3,2,0,1:T(8,128)(2,1)S(1)}, u32[]{:S(2)}, u32[]{:S(2)}) collective-permute-start(bf16[2,2,32,1792]{3,2,0,1:T(8,128)(2,1)S(1)} %dynamic-slice_bitcast_fusion), channel_id=1, source_target_pairs={{0,2},{2,0},{4,6},{6,4},{8,10},{10,8},{12,14},{14,12},{16,18},{18,... | collective-permute-start | bytes 1376264 | tf_op jit(solution)/shard_map/ppermute | solution.py:250
  337.1 11.8 %collective-permute-start.1 = (bf16[2,2,32,1792]{3,2,0,1:T(8,128)(2,1)S(1)}, bf16[2,2,32,1792]{3,2,0,1:T(8,128)(2,1)S(1)}, u32[]{:S(2)}, u32[]{:S(2)}) collective-permute-start(bf16[2,2,32,1792]{3,2,0,1:T(8,128)(2,1)S(1)} %dynamic-slice_bitcast_fusion.1), channel_id=1, source_target_pairs={{0,4},{2,6},{4,0},{6,2},{8,12},{10,14},{12,8},{14,10},{16,20},{18,... | collective-permute-start | bytes 1376264 | tf_op jit(solution)/shard_map/ppermute | solution.py:250
  349.1 10.9 %collective-permute-start.4 = (bf16[2,32,3584]{2,1,0:T(8,128)(2,1)S(1)}, bf16[2,32,3584]{2,1,0:T(8,128)(2,1)S(1)}, u32[]{:S(2)}, u32[]{:S(2)}) collective-permute-start(bf16[2,32,3584]{2,1,0:T(8,128)(2,1)S(1)} %fusion.55), channel_id=1, source_target_pairs={{0,8},{2,10},{4,12},{6,14},{8,0},{10,2},{12,4},{14,6},{16,24},{18,... | collective-permute-start | bytes 1376264 | tf_op jit(solution)/shard_map/ppermute | solution.py:250
  360.2 10.9 %collective-permute-start.5 = (bf16[32,3584]{1,0:T(8,128)(2,1)S(1)}, bf16[32,3584]{1,0:T(8,128)(2,1)S(1)}, u32[]{:S(2)}, u32[]{:S(2)}) collective-permute-start(bf16[32,3584]{1,0:T(8,128)(2,1)S(1)} %dynamic-slice_bitcast_fusion.2), channel_id=1, source_target_pairs={{0,16},{2,18},{4,20},{6,22},{8,24},{10,26},{12,28},{14,30},{16,0},... | collective-permute-start | bytes 688136 | tf_op jit(solution)/shard_map/ppermute | solution.py:250
Sparse Core Ops, SparseCore 0:
  216.0 6.0 reduce-scatter.2
  289.5 16.0 reduce-scatter.4

commit v3 on v2

--- a/solution.py
+++ b/solution.py
@@ -251,14 +251,32 @@
     return (keep.astype(F32) + got.astype(F32)).astype(values.dtype)
 
 
-def scatter_sum(values, rows):
-    width = values.shape[1]
-    split = values.reshape(2, 2, 2, 2, rows, width)
-    first, second = split[..., : width // 2], split[..., width // 2:]
+def scatter_experts(hidden, weight, gate, rows):
+    core = lax.axis_index("mp")
+    width = weight.shape[1] // 2
+    last = 2 * width // 7
+    size = (width - last) // 2
+
+    def product(owner, start, count):
+        columns = lax.dynamic_slice_in_dim(weight, owner * width + start, count, 1)
+        return (jnp.dot(hidden, columns, preferred_element_type=F32) * gate[:, None]).astype(BF16)
+
+    def summed(start, count):
+        got = lax.ppermute(product(1 - core, start, count), "mp", [(0, 1), (1, 0)])
+        kept = product(core, start, count)
+        total = (kept.astype(F32) + got.astype(F32)).astype(BF16)
+        return total.reshape(2, 2, 2, 2, rows, count)
+
+    third = summed(2 * size, last)
+    first = summed(0, size)
+    second = summed(size, size)
+    third = fold(fold(third, 1, 4), 0, 8)
     first = fold(fold(first, 3, 1), 2, 2)
     second = fold(fold(second, 2, 2), 2, 1)
+    third = fold(fold(third, 1, 1), 0, 2)
     both = jnp.concatenate([first, second], axis=-1)
-    return fold(fold(both, 1, 4), 0, 8)
+    both = fold(fold(both, 1, 4), 0, 8)
+    return jnp.concatenate([both, third], axis=-1)
 
 
 def local(
@@ -310,22 +328,33 @@
     own_slot = parent_of * pair_slots + own_rank
     placer = (jnp.arange(slots_total, dtype=I32)[:, None] == own_slot[None, :]).astype(BF16)
 
-    query_cols = new_tokens * heads_here * query_width
-    payload = jnp.concatenate(
-        [queries.reshape(children_here, -1), new_latents.reshape(children_here, -1)], axis=1
-    )
-    outgoing = jnp.dot(placer, payload, preferred_element_type=F32).astype(BF16)
-    arrived = lax.all_to_all(outgoing, "search", split_axis=0, concat_axis=0, tiled=True)
-    held = jnp.dot(picker, arrived, preferred_element_type=F32).astype(BF16)
-    held_query = held[:, :query_cols].reshape(children_here, new_tokens, heads_here, query_width)
-    held_latents = held[:, query_cols:].reshape(children_here, new_tokens, kv_width)
-
-    latent_query = jnp.einsum(
-        "cthn,hnl->cthl", held_query[..., :nope_width], up_keys, preferred_element_type=F32
-    ).astype(BF16)
-    full_query = jnp.concatenate([latent_query, held_query[..., nope_width:]], axis=-1)
-    latent_out = attend(full_query, held_latents, parent_cache[0], latent_width, softmax_scale)
-    head_out = jnp.einsum("cthl,hlv->cthv", latent_out, up_values, preferred_element_type=F32).astype(BF16)
+    heads_part = heads_here // 2
+    query_cols = new_tokens * heads_part * query_width
+    head_outs, arrived, held_latents = [], None, None
+    for part in range(2):
+        heads = slice(part * heads_part, (part + 1) * heads_part)
+        payload = queries[:, :, heads].reshape(children_here, -1)
+        if part == 0:
+            payload = jnp.concatenate([payload, new_latents.reshape(children_here, -1)], axis=1)
+        outgoing = jnp.dot(placer, payload, preferred_element_type=F32).astype(BF16)
+        if part == 1:
+            outgoing, arrived = lax.optimization_barrier((outgoing, arrived))
+        arrived = lax.all_to_all(outgoing, "search", split_axis=0, concat_axis=0, tiled=True)
+        held = jnp.dot(picker, arrived, preferred_element_type=F32).astype(BF16)
+        held_query = held[:, :query_cols].reshape(children_here, new_tokens, heads_part, query_width)
+        if part == 0:
+            held_latents = held[:, query_cols:].reshape(children_here, new_tokens, kv_width)
+        latent_query = jnp.einsum(
+            "cthn,hnl->cthl", held_query[..., :nope_width], up_keys[heads], preferred_element_type=F32
+        ).astype(BF16)
+        full_query = jnp.concatenate([latent_query, held_query[..., nope_width:]], axis=-1)
+        latent_out = attend(full_query, held_latents, parent_cache[0], latent_width, softmax_scale)
+        head_outs.append(
+            jnp.einsum(
+                "cthl,hlv->cthv", latent_out, up_values[heads], preferred_element_type=F32
+            ).astype(BF16)
+        )
+    head_out = jnp.concatenate(head_outs, axis=2)
     attention = head_out.reshape(token_rows, heads_here * value_width)
 
     block_4x2x2 = searchers == 16 and lax.axis_size("mp") == 2
@@ -378,12 +407,12 @@
         gate_act += jnp.dot(slices[part], w_gate[0, span], preferred_element_type=F32)
         up_act += jnp.dot(slices[part], w_up[0, span], preferred_element_type=F32)
     expert_hidden = (jax.nn.silu(gate_act) * up_act).astype(BF16)
-    expert_part = jnp.dot(expert_hidden, w_down[0], preferred_element_type=F32)
-    weighted = (expert_part * my_gate[:, None]).astype(BF16)
-    weighted = lax.psum_scatter(weighted, "mp", scatter_dimension=1, tiled=True)
     if block_4x2x2:
-        expert_mix = scatter_sum(weighted, token_rows).astype(F32)
+        expert_mix = scatter_experts(expert_hidden, w_down[0], my_gate, token_rows).astype(F32)
     else:
+        expert_part = jnp.dot(expert_hidden, w_down[0], preferred_element_type=F32)
+        weighted = (expert_part * my_gate[:, None]).astype(BF16)
+        weighted = lax.psum_scatter(weighted, "mp", scatter_dimension=1, tiled=True)
         expert_mix = lax.psum_scatter(weighted, "search", scatter_dimension=0, tiled=True).astype(F32)
     mixed = (residual_wide + expert_mix).astype(BF16)
     return mixed.reshape(children_here, new_tokens, width_here)

time: 379 us -> 359 us (0.947); the launches traced: 379 us -> 354 us
  waiting for transfers between devices: 68.6 us -> 47.5 us
  blocking collectives: 49.9 us -> 34.7 us
  matrix products: 41.3 us -> 52.7 us
  starting transfers between devices: 18.2 us -> 24.9 us
  local copies, waits for them, and re-layouts: 32.4 us -> 27.9 us
    reduce_scatter x1 -> x0, waiting for transfers between devices: 16.2 us -> none  [local(): weighted = lax.psum_scatter(weighted, 'mp', scatter_dimension=1, tiled=True)]
    unnamed x1, blocking collectives: 29.5 us -> 14.9 us
    dot_general x3 -> x10, matrix products: 16.8 us -> 27.8 us  [the longest x6 15.4 us: product(): jnp.dot(hidden, columns, preferred_element_type=F32) * gate[:, None]]
    ppermute x6 -> x10, waiting for transfers between devices: 46.5 us -> 41.4 us  [fold(): lax.ppermute(give, 'search', [(i, i ^ distance) for i in range(count)])]
    all_to_all x1 -> x2, starting transfers between devices: 8.31 us -> 11.9 us  [local(): lax.all_to_all(outgoing, 'search', split_axis=0, concat_axis=0, tiled=True)]
    unnamed x35 -> x26, local copies, waits for them, and re-layouts: 13.2 us -> 10.1 us
    pallas_call x1 -> x2, Pallas kernels: 33.7 us -> 36 us  [attend(): pl.pallas_call(body, grid=(tiles,), in_specs=[pl.BlockSpec((rows, kv_widt...]
    ppermute x6 -> x10, starting transfers between devices: 9.84 us -> 11.8 us  [fold(): lax.ppermute(give, 'search', [(i, i ^ distance) for i in range(count)])]
  transfers between devices with their start and end apart: 9 -> 16, of which waited for: 8 -> 7; matrix products, arithmetic and copies ran while one was open for 4% -> 9% of each run, Pallas kernels for 0% -> 5%
where the time goes in v3:
time: 359 us; the launch traced here: 354 us
  Pallas kernels  145 us (40%)
  matrix products  52.7 us (15%)
  waiting for transfers between devices  47.5 us (13%)
  blocking collectives  34.7 us (10%)
  local copies, waits for them, and re-layouts  27.9 us (8%)
  starting transfers between devices  24.9 us (7%)
  between operations  15 us (4%)
  other arithmetic  6.36 us (2%)
    pallas_call x2, Pallas kernels, gather_blocks(): pl.pallas_call(functools.partial(gather_kernel, across), out_shape=jax.Sh...  109 us
    ppermute x10, waiting for transfers between devices, fold(): lax.ppermute(give, 'search', [(i, i ^ distance) for i in range(count)])  41.4 us
    pallas_call x2, Pallas kernels, attend(): pl.pallas_call(body, grid=(tiles,), in_specs=[pl.BlockSpec((rows, kv_widt...  36 us
    all_to_all x1, blocking collectives, local(): lax.all_to_all(every_row, 'search', split_axis=0, concat_axis=1, tiled=True)  16.4 us
    dot_general x6, matrix products, product(): jnp.dot(hidden, columns, preferred_element_type=F32) * gate[:, None]  15.4 us
    unnamed x1, blocking collectives  14.9 us
    all_to_all x2, starting transfers between devices, local(): lax.all_to_all(outgoing, 'search', split_axis=0, concat_axis=0, tiled=True)  11.9 us
    ppermute x10, starting transfers between devices, fold(): lax.ppermute(give, 'search', [(i, i ^ distance) for i in range(count)])  11.8 us
  transfers between devices with their start and end apart: 16, of which 7 were waited for; matrix products, arithmetic and copies ran while one was open for 9% of the time, Pallas kernels for 5%

profile of v3, /device:TPU:0, one launch (start us, length us, event | category | flops | bytes accessed | tf_op | source)
XLA Modules:
  0.0 354.2 jit_solution(10868844493948469834)
XLA Ops:
  12.5 8.3 %all-to-all-start = ((bf16[16,2,13440]{2,1,0:T(2,128)(2,1)}), bf16[16,2,13440]{2,1,0:T(2,128)(2,1)S(1)}, u32[]{:S(2)}, u32[]{:S(2)}) async-start(bf16[16,2,13440]{2,1,0:T(2,128)(2,1)} %all_to_all.28), calls=%async_computation | async-start | bytes 1720320 | tf_op jit(solution)/shard_map/all_to_all | solution.py:342
  21.4 7.7 %copy.74 = bf16[1,4096,576]{2,1,0:T(8,128)(2,1)} copy(bf16[1,4096,576]{1,2,0:T(8,128)(2,1)} %param.15) | data formatting | bytes 9437184 | tf_op args[2]
  30.6 14.9 %all-reduce = s32[256]{0:T(256)S(1)} all-reduce(s32[256]{0:T(256)S(1)} %dynamic-update-slice), channel_id=1, replica_groups=mesh['search'=16,'mp'=2] {'search'}, use_global_device_ids=true, to_apply=%add | all-reduce | flops 256 | bytes 2048
  48.3 3.6 %all-to-all-start.1 = ((bf16[16,2,12288]{2,1,0:T(2,128)(2,1)}), bf16[16,2,12288]{2,1,0:T(2,128)(2,1)S(1)}, u32[]{:S(2)}, u32[]{:S(2)}) async-start(bf16[16,2,12288]{2,1,0:T(2,128)(2,1)} %all_to_all.31), calls=%async_computation.1 | async-start | bytes 1572864 | tf_op jit(solution)/shard_map/all_to_all | solution.py:342
  53.2 3.0 fusion.39
  58.2 17.8 %attend.2 = bf16[1024,512]{1,0:T(8,128)(2,1)S(1)} custom-call(bf16[1024,576]{1,0:T(8,128)(2,1)} %bitcast.223, bf16[2,16,576]{2,1,0:T(8,128)(2,1)S(1)} %reshape_reshape.4.own_ref, bf16[4096,576]{1,0:T(8,128)(2,1)} %bitcast.215), custom_call_target="tpu_custom_call" | custom-call | flops 9126805504 | bytes 6946816 | tf_op jit(solution)/shard_map/attend/pallas_call | solution.py:58
  76.0 3.2 fusion.77
  80.6 3.0 fusion.36
  85.4 18.2 %attend.3 = bf16[1024,512]{1,0:T(8,128)(2,1)S(1)} custom-call(bf16[1024,576]{1,0:T(8,128)(2,1)} %bitcast.222, bf16[2,16,576]{2,1,0:T(8,128)(2,1)S(1)} %reshape_reshape.4.own_ref, bf16[4096,576]{1,0:T(8,128)(2,1)} %bitcast.216), custom_call_target="tpu_custom_call" | custom-call | flops 9126805504 | bytes 6946816 | tf_op jit(solution)/shard_map/attend/pallas_call | solution.py:58
  103.6 3.2 fusion.74
  108.3 69.4 %gather_heads.1 = bf16[16,32,8192]{2,1,0:T(8,128)(2,1)} custom-call(bf16[32,8192]{1,0:T(8,128)(2,1)} %bitcast.217), custom_call_target="tpu_custom_call" | custom-call | tf_op jit(solution)/shard_map/gather_heads/pallas_call | solution.py:228
  177.8 9.4 %convolution_convert_fusion.4 = bf16[512,448]{0,1:T(8,128)(2,1)S(1)} fusion(bf16[512,8192]{1,0:T(8,128)(2,1)} %bitcast.207, bf16[8192,448]{0,1:T(8,128)(2,1)} %param.19), kind=kOutput, calls=%fused_computation.68 | convolution fusion | flops 3758325760 | bytes 16187392 | tf_op jit(solution)/shard_map/dot_general | solution.py:365
  189.5 16.4 %all_to_all.40 = bf16[16,32,448]{2,1,0:T(8,128)(2,1)S(1)} all-to-all(bf16[16,32,448]{2,1,0:T(8,128)(2,1)S(1)} %broadcast_select_fusion), channel_id=1, replica_groups=mesh['search'=16,'mp'=2] {'search'}, dimensions={0} | all-to-all | bytes 917504 | tf_op jit(solution)/shard_map/all_to_all | solution.py:370
  208.0 6.1 %reduce-scatter.2.cloned.1.call-done = bf16[32,3584]{1,0:T(8,128)(2,1)} async-done(((bf16[32,7168]{1,0:T(8,128)(2,1)}), bf16[32,3584]{1,0:T(8,128)(2,1)}) %reduce-scatter.2.cloned.1.call-update) | async-done | bytes 229392 | tf_op jit(solution)/shard_map/reduce_scatter | solution.py:371
  215.3 3.4 all-reduce.1
  220.0 39.7 %gather_tokens.1 = bf16[2,16,32,3712]{3,2,1,0:T(8,128)(2,1)} custom-call(bf16[32,3712]{1,0:T(8,128)(2,1)} %concatenate.25.x_ref), custom_call_target="tpu_custom_call" | custom-call | tf_op jit(solution)/shard_map/gather_tokens/pallas_call | solution.py:228
  260.7 5.4 %fusion.16 = f32[512,512]{1,0:T(8,128)S(1)} fusion(bf16[1,7168,512]{2,1,0:T(8,128)(2,1)} %param.23, bf16[2,512,3712]{2,1,0:T(8,128)(2,1)} %bitcast.209), kind=kOutput, calls=%fused_computation.23 | convolution fusion | flops 1879048192 | bytes 8388608 | tf_op jit(solution)/shard_map/dot_general | solution.py:407
  266.2 4.2 %fusion.42 = f32[512,512]{1,0:T(8,128)S(1)} fusion(f32[512,512]{1,0:T(8,128)S(1)} %fusion.16, bf16[1,7168,512]{2,1,0:T(8,128)(2,1)} %param.23, bf16[2,512,3712]{2,1,0:T(8,128)(2,1)S(1)} %bitcast.212), kind=kOutput, calls=%fused_computation.50 | convolution fusion | flops 1879310336 | bytes 9437184 | tf_op jit(solution)/shard_map/dot_general | solution.py:407
  272.6 2.2 fusion.65
  275.0 3.0 multiply_convert_fusion
  278.3 3.3 fusion.29
  281.7 2.2 fusion.26
  284.3 2.3 add_convert_fusion.2
  287.0 2.6 add_convert_fusion
  291.3 2.2 add_convert_fusion.1
  293.4 7.4 %collective-permute-done.9 = bf16[2,2,2,32,1024]{4,3,1,2,0:T(8,128)(2,1)S(1)} collective-permute-done((bf16[2,2,2,32,1024]{4,3,1,2,0:T(8,128)(2,1)S(1)}, bf16[2,2,2,32,1024]{4,3,1,2,0:T(8,128)(2,1)S(1)}, u32[]{:S(2)}, u32[]{:S(2)}) %collective-permute-start.9) | collective-permute-done | bytes 524320 | tf_op jit(solution)/shard_map/ppermute | solution.py:250
  301.1 2.7 collective-permute-start.10
  304.8 10.6 %collective-permute-done.10 = bf16[2,2,32,1024]{3,2,0,1:T(8,128)(2,1)S(1)} collective-permute-done((bf16[2,2,32,1024]{3,2,0,1:T(8,128)(2,1)S(1)}, bf16[2,2,32,1024]{3,2,0,1:T(8,128)(2,1)S(1)}, u32[]{:S(2)}, u32[]{:S(2)}) %collective-permute-start.10) | collective-permute-done | bytes 262176 | tf_op jit(solution)/shard_map/ppermute | solution.py:250
  317.9 3.7 %collective-permute-done.1 = bf16[2,2,2,32,1280]{4,3,0,1,2:T(8,128)(2,1)S(1)} collective-permute-done((bf16[2,2,2,32,1280]{4,3,0,1,2:T(8,128)(2,1)S(1)}, bf16[2,2,2,32,1280]{4,3,0,1,2:T(8,128)(2,1)S(1)}, u32[]{:S(2)}, u32[]{:S(2)}) %collective-permute-start.1) | collective-permute-done | bytes 655392 | tf_op jit(solution)/shard_map/ppermute | solution.py:250
  322.7 7.0 %collective-permute-done.5 = bf16[2,2,32,1280]{3,2,0,1:T(8,128)(2,1)S(1)} collective-permute-done((bf16[2,2,32,1280]{3,2,0,1:T(8,128)(2,1)S(1)}, bf16[2,2,32,1280]{3,2,0,1:T(8,128)(2,1)S(1)}, u32[]{:S(2)}, u32[]{:S(2)}) %collective-permute-start.5) | collective-permute-done | bytes 327712 | tf_op jit(solution)/shard_map/ppermute | solution.py:250
  332.2 5.9 %collective-permute-done.6 = bf16[2,32,2560]{2,1,0:T(8,128)(2,1)S(1)} collective-permute-done((bf16[2,32,2560]{2,1,0:T(8,128)(2,1)S(1)}, bf16[2,32,2560]{2,1,0:T(8,128)(2,1)S(1)}, u32[]{:S(2)}, u32[]{:S(2)}) %collective-permute-start.6) | collective-permute-done | bytes 327712 | tf_op jit(solution)/shard_map/ppermute | solution.py:250
  339.6 6.7 %collective-permute-done.7 = bf16[32,2560]{1,0:T(8,128)(2,1)S(1)} collective-permute-done((bf16[32,2560]{1,0:T(8,128)(2,1)S(1)}, bf16[32,2560]{1,0:T(8,128)(2,1)S(1)}, u32[]{:S(2)}, u32[]{:S(2)}) %collective-permute-start.7) | collective-permute-done | bytes 163872 | tf_op jit(solution)/shard_map/ppermute | solution.py:250
  (140 shorter events, 40.5 us)
Async XLA Ops:
  6.5 208.6 %copy-start = (bf16[3584,16]{0,1:T(8,128)(2,1)S(1)}, bf16[3584,16]{0,1:T(8,128)(2,1)}, u32[]{:S(2)}) copy-start(bf16[3584,16]{0,1:T(8,128)(2,1)} %param.21) | copy-start | bytes 344068
  12.5 34.1 %all-to-all-start = ((bf16[16,2,13440]{2,1,0:T(2,128)(2,1)}), bf16[16,2,13440]{2,1,0:T(2,128)(2,1)S(1)}, u32[]{:S(2)}, u32[]{:S(2)}) async-start(bf16[16,2,13440]{2,1,0:T(2,128)(2,1)} %all_to_all.28), calls=%async_computation | async-start | bytes 1720320 | tf_op jit(solution)/shard_map/all_to_all | solution.py:342
  21.4 7.7 %copy-start.4 = (u32[32]{0:T(128)S(1)}, u32[32]{0:T(128)}, u32[]{:S(2)}) copy-start(u32[32]{0:T(128)} %constant.193) | copy-start | bytes 388
  21.4 8.9 %copy-start.3 = (s32[16]{0:T(128)S(1)}, s32[16]{0:T(128)}, u32[]{:S(2)}) copy-start(s32[16]{0:T(128)} %param.16) | copy-start | bytes 196
  48.3 30.9 %all-to-all-start.1 = ((bf16[16,2,12288]{2,1,0:T(2,128)(2,1)}), bf16[16,2,12288]{2,1,0:T(2,128)(2,1)S(1)}, u32[]{:S(2)}, u32[]{:S(2)}) async-start(bf16[16,2,12288]{2,1,0:T(2,128)(2,1)} %all_to_all.31), calls=%async_computation.1 | async-start | bytes 1572864 | tf_op jit(solution)/shard_map/all_to_all | solution.py:342
  51.9 162.1 %reduce-scatter.2.cloned.1.call-start = ((), (), s32[]{:S(2)}) async-start(), calls=%async_computation.4 | async-start | bytes 688128 | tf_op jit(solution)/shard_map/reduce_scatter | solution.py:371
  189.0 18.6 %copy-start.1 = (bf16[16,2,3584]{2,1,0:T(2,128)(2,1)S(1)}, bf16[16,2,3584]{2,1,0:T(2,128)(2,1)}, u32[]{:S(2)}) copy-start(bf16[16,2,3584]{2,1,0:T(2,128)(2,1)} %param.20) | copy-start | bytes 688132
  189.0 18.7 %copy-start.2 = (s32[16,2,8]{0,2,1:T(8,128)S(1)}, s32[16,2,8]{0,2,1:T(8,128)}, u32[]{:S(2)}) copy-start(s32[16,2,8]{0,2,1:T(8,128)} %param.22) | copy-start | bytes 3076
  259.6 6.6 %slice-start = ((s8[7602176]{0:T(1024)(128)(4,1)}), s8[4194304]{0:T(1024)(128)(4,1)S(1)}, s32[]{:S(2)}) async-start(s8[7602176]{0:T(1024)(128)(4,1)} %bitcast.210), calls=%async_computation.5 | async-start | bytes 8388608
  260.7 5.5 %slice-start.1 = ((s8[7602176]{0:T(1024)(128)(4,1)}), s8[3407872]{0:T(1024)(128)(4,1)S(1)}, s32[]{:S(2)}) async-start(s8[7602176]{0:T(1024)(128)(4,1)} %bitcast.210), calls=%async_computation.6 | async-start | bytes 6815744
  260.7 9.8 %slice-start.2 = ((s8[7340032]{0:T(1024)(128)(4,1)}), s8[4194304]{0:T(1024)(128)(4,1)S(1)}, s32[]{:S(2)}) async-start(s8[7340032]{0:T(1024)(128)(4,1)} %bitcast.229), calls=%async_computation.7 | async-start | bytes 8388608
  266.2 4.3 %slice-start.3 = ((s8[7340032]{0:T(1024)(128)(4,1)}), s8[3145728]{0:T(1024)(128)(4,1)S(1)}, s32[]{:S(2)}) async-start(s8[7340032]{0:T(1024)(128)(4,1)} %bitcast.229), calls=%async_computation.8 | async-start | bytes 6291456
  278.0 6.4 %collective-permute-start.8 = (bf16[512,1024]{1,0:T(8,128)(2,1)}, bf16[512,1024]{1,0:T(8,128)(2,1)}, u32[]{:S(2)}, u32[]{:S(2)}) collective-permute-start(bf16[512,1024]{1,0:T(8,128)(2,1)} %multiply_convert_fusion), channel_id=1, source_target_pairs={{0,1},{1,0},{2,3},{3,2},{4,5},{5,4},{6,7},{7,6},{8,9},{9,8},{10,11... | collective-permute-start | bytes 3145736 | tf_op jit(solution)/shard_map/ppermute | solution.py:265
  281.6 5.4 %collective-permute-start.3 = (bf16[512,1280]{1,0:T(8,128)(2,1)}, bf16[512,1280]{1,0:T(8,128)(2,1)}, u32[]{:S(2)}, u32[]{:S(2)}) collective-permute-start(bf16[512,1280]{1,0:T(8,128)(2,1)} %fusion.29), channel_id=1, source_target_pairs={{0,1},{1,0},{2,3},{3,2},{4,5},{5,4},{6,7},{7,6},{8,9},{9,8},{10,11... | collective-permute-start | bytes 3932168 | tf_op jit(solution)/shard_map/ppermute | solution.py:265
  283.9 7.4 %collective-permute-start = (bf16[512,1280]{1,0:T(8,128)(2,1)S(1)}, bf16[512,1280]{1,0:T(8,128)(2,1)S(1)}, u32[]{:S(2)}, u32[]{:S(2)}) collective-permute-start(bf16[512,1280]{1,0:T(8,128)(2,1)S(1)} %fusion.26), channel_id=1, source_target_pairs={{0,1},{1,0},{2,3},{3,2},{4,5},{5,4},{6,7},{7,6},{8,9},{9,8},{10,11... | collective-permute-start | bytes 3932168 | tf_op jit(solution)/shard_map/ppermute | solution.py:265
  286.8 14.0 %collective-permute-start.9 = (bf16[2,2,2,32,1024]{4,3,1,2,0:T(8,128)(2,1)S(1)}, bf16[2,2,2,32,1024]{4,3,1,2,0:T(8,128)(2,1)S(1)}, u32[]{:S(2)}, u32[]{:S(2)}) collective-permute-start(bf16[2,2,2,32,1024]{4,3,1,2,0:T(8,128)(2,1)S(1)} %bitcast.227), channel_id=1, source_target_pairs={{0,8},{2,10},{4,12},{6,14},{8,0},{10,2},{12,4},{14,6},{16,24},{18,... | collective-permute-start | bytes 1572872 | tf_op jit(solution)/shard_map/ppermute | solution.py:250
  289.7 26.6 %collective-permute-start.4 = (bf16[2,2,2,32,1280]{4,3,0,1,2:T(8,128)(2,1)S(1)}, bf16[2,2,2,32,1280]{4,3,0,1,2:T(8,128)(2,1)S(1)}, u32[]{:S(2)}, u32[]{:S(2)}) collective-permute-start(bf16[2,2,2,32,1280]{4,3,0,1,2:T(8,128)(2,1)S(1)} %bitcast.225), channel_id=1, source_target_pairs={{0,4},{2,6},{4,0},{6,2},{8,12},{10,14},{12,8},{14,10},{16,20},{18,... | collective-permute-start | bytes 1966088 | tf_op jit(solution)/shard_map/ppermute | solution.py:250
  301.1 14.4 %collective-permute-start.10 = (bf16[2,2,32,1024]{3,2,0,1:T(8,128)(2,1)S(1)}, bf16[2,2,32,1024]{3,2,0,1:T(8,128)(2,1)S(1)}, u32[]{:S(2)}, u32[]{:S(2)}) collective-permute-start(bf16[2,2,32,1024]{3,2,0,1:T(8,128)(2,1)S(1)} %dynamic-slice_bitcast_fusion.2), channel_id=1, source_target_pairs={{0,16},{2,18},{4,20},{6,22},{8,24},{10,26},{12,28},{14,30},{16,0},... | collective-permute-start | bytes 786440 | tf_op jit(solution)/shard_map/ppermute | solution.py:250
  303.9 17.7 %collective-permute-start.1 = (bf16[2,2,2,32,1280]{4,3,0,1,2:T(8,128)(2,1)S(1)}, bf16[2,2,2,32,1280]{4,3,0,1,2:T(8,128)(2,1)S(1)}, u32[]{:S(2)}, u32[]{:S(2)}) collective-permute-start(bf16[2,2,2,32,1280]{4,3,0,1,2:T(8,128)(2,1)S(1)} %bitcast.226), channel_id=1, source_target_pairs={{0,2},{2,0},{4,6},{6,4},{8,10},{10,8},{12,14},{14,12},{16,18},{18,... | collective-permute-start | bytes 1966088 | tf_op jit(solution)/shard_map/ppermute | solution.py:250
  315.5 15.9 %collective-permute-start.11 = (bf16[2,32,1024]{2,1,0:T(8,128)(2,1)S(1)}, bf16[2,32,1024]{2,1,0:T(8,128)(2,1)S(1)}, u32[]{:S(2)}, u32[]{:S(2)}) collective-permute-start(bf16[2,32,1024]{2,1,0:T(8,128)(2,1)S(1)} %dynamic-slice_bitcast_fusion.4), channel_id=1, source_target_pairs={{0,2},{2,0},{4,6},{6,4},{8,10},{10,8},{12,14},{14,12},{16,18},{18,... | collective-permute-start | bytes 393224 | tf_op jit(solution)/shard_map/ppermute | solution.py:250
  316.5 13.3 %collective-permute-start.5 = (bf16[2,2,32,1280]{3,2,0,1:T(8,128)(2,1)S(1)}, bf16[2,2,32,1280]{3,2,0,1:T(8,128)(2,1)S(1)}, u32[]{:S(2)}, u32[]{:S(2)}) collective-permute-start(bf16[2,2,32,1280]{3,2,0,1:T(8,128)(2,1)S(1)} %dynamic-slice_bitcast_fusion), channel_id=1, source_target_pairs={{0,2},{2,0},{4,6},{6,4},{8,10},{10,8},{12,14},{14,12},{16,18},{18,... | collective-permute-start | bytes 983048 | tf_op jit(solution)/shard_map/ppermute | solution.py:250
  321.8 8.0 %collective-permute-start.2 = (bf16[2,2,32,1280]{3,2,0,1:T(8,128)(2,1)S(1)}, bf16[2,2,32,1280]{3,2,0,1:T(8,128)(2,1)S(1)}, u32[]{:S(2)}, u32[]{:S(2)}) collective-permute-start(bf16[2,2,32,1280]{3,2,0,1:T(8,128)(2,1)S(1)} %dynamic-slice_bitcast_fusion.1), channel_id=1, source_target_pairs={{0,4},{2,6},{4,0},{6,2},{8,12},{10,14},{12,8},{14,10},{16,20},{18,... | collective-permute-start | bytes 983048 | tf_op jit(solution)/shard_map/ppermute | solution.py:250
  330.0 8.1 %collective-permute-start.6 = (bf16[2,32,2560]{2,1,0:T(8,128)(2,1)S(1)}, bf16[2,32,2560]{2,1,0:T(8,128)(2,1)S(1)}, u32[]{:S(2)}, u32[]{:S(2)}) collective-permute-start(bf16[2,32,2560]{2,1,0:T(8,128)(2,1)S(1)} %fusion.98), channel_id=1, source_target_pairs={{0,8},{2,10},{4,12},{6,14},{8,0},{10,2},{12,4},{14,6},{16,24},{18,... | collective-permute-start | bytes 983048 | tf_op jit(solution)/shard_map/ppermute | solution.py:250
  331.5 8.0 %collective-permute-start.12 = (bf16[32,1024]{1,0:T(8,128)(2,1)S(1)}, bf16[32,1024]{1,0:T(8,128)(2,1)S(1)}, u32[]{:S(2)}, u32[]{:S(2)}) collective-permute-start(bf16[32,1024]{1,0:T(8,128)(2,1)S(1)} %dynamic-slice_bitcast_fusion.5), channel_id=1, source_target_pairs={{0,4},{2,6},{4,0},{6,2},{8,12},{10,14},{12,8},{14,10},{16,20},{18,... | collective-permute-start | bytes 196616 | tf_op jit(solution)/shard_map/ppermute | solution.py:250
  338.2 8.1 %collective-permute-start.7 = (bf16[32,2560]{1,0:T(8,128)(2,1)S(1)}, bf16[32,2560]{1,0:T(8,128)(2,1)S(1)}, u32[]{:S(2)}, u32[]{:S(2)}) collective-permute-start(bf16[32,2560]{1,0:T(8,128)(2,1)S(1)} %dynamic-slice_bitcast_fusion.3), channel_id=1, source_target_pairs={{0,16},{2,18},{4,20},{6,22},{8,24},{10,26},{12,28},{14,30},{16,0},... | collective-permute-start | bytes 491528 | tf_op jit(solution)/shard_map/ppermute | solution.py:250
Sparse Core Ops, SparseCore 0:
  207.7 6.2 reduce-scatter.1
